TPU v7x, 32 devices: a whole 2x2x4 slice. The times are simulated.
32 devices in a mesh: leaf: 2 (over y), frow: 4 (over z), fcol: 4 (over x, core).
Axes of the slice: x: 2, y: 2, z: 4, core: 2. Of those that a mesh axis runs over, the one named last changes fastest.
Arguments:
- child_fronts: float32 [2, 4096, 4096], P('leaf', 'frow', 'fcol'), may hold values from -20 to 120, as said below
- parent_front: float32 [4096, 4096], P('frow', 'fcol'), may hold values from -20 to 120, as said below
- block_maps: int32 [2, 32], P('leaf'), may hold values from 0 to 31, as said below
Outputs:
- child_factors: float32 [2, 4096, 4096], P('leaf', 'frow', 'fcol')
- parent_factor: float32 [4096, 4096], P('frow', 'fcol')
Inputs may be any that keep to these rules, and one draw needn't show every extreme that they name: Each row block_maps[l] is a permutation of the block numbers that keeps every block inside its group of 8 consecutive blocks: block_maps[l, i] // 8 == i // 8. `child_fronts`: every child front is symmetric positive definite. `parent_front`: the parent front is symmetric positive definite.
All inputs are finite; a program needn't handle non-finite values.
Results may differ from a plain program's by a relative error of at most 0.0001.
Values sent between devices are 32-bit elements; how exact they have to be, the bound alone decides.
A program may use at most 64 MiB of HBM per device.

v0:
```python
import jax
import jax.numpy as jnp
from jax import lax
from jax.sharding import PartitionSpec as P

BLOCK = 128
CHILD_PANELS = 2
PARENT_PANELS = 1


def from_root(shard, axis, root):
    mine = lax.axis_index(axis) == root
    return lax.psum(jnp.where(mine, shard, jnp.zeros_like(shard)), axis)


def factor_panels(matrix, row_start, col_start, panels, diag_share, panel_share, column_share):
    height, breadth = matrix.shape
    global_rows = row_start + jnp.arange(height, dtype=jnp.int32)
    global_cols = col_start + jnp.arange(breadth, dtype=jnp.int32)
    inside = row_start // breadth == col_start // breadth
    offset = jnp.clip(row_start - col_start, 0, breadth - height)
    for number in range(panels):
        first_col = number * BLOCK
        end_col = first_col + BLOCK
        owner_col = first_col // breadth
        within = first_col - owner_col * breadth
        holder = col_start // breadth == owner_col
        column = matrix[:, within : within + BLOCK]
        pivot_block = diag_share(column, first_col)
        pivot_block = jnp.where(holder, pivot_block, jnp.eye(BLOCK, dtype=jnp.float32))
        factor = jnp.linalg.cholesky(pivot_block)
        solved = lax.linalg.triangular_solve(
            factor, column, left_side=False, lower=True, transpose_a=True
        )
        picked = jnp.take(factor, jnp.clip(global_rows - first_col, 0, BLOCK - 1), axis=0)
        before = (global_rows < first_col)[:, None]
        middle = (global_rows < end_col)[:, None]
        own_panel = jnp.where(before, 0.0, jnp.where(middle, picked, solved))
        shared = panel_share(own_panel, owner_col)
        framed = lax.dynamic_update_slice(
            jnp.zeros((breadth, BLOCK), jnp.float32), jnp.where(inside, shared, 0.0), (offset, 0)
        )
        across = column_share(framed)
        update = jnp.dot(shared, across.T, precision=lax.Precision.HIGHEST)
        later_cols = (global_cols >= end_col)[None, :]
        trailing = (global_rows >= end_col)[:, None] & later_cols
        pivot_rows = ((global_rows >= first_col) & (global_rows < end_col))[:, None] & later_cols
        matrix = jnp.where(trailing, matrix - update, jnp.where(pivot_rows, 0.0, matrix))
        current = matrix[:, within : within + BLOCK]
        matrix = matrix.at[:, within : within + BLOCK].set(jnp.where(holder, shared, current))
    return matrix


def block_inverse(targets, base, members):
    local_target = targets - base
    slot_index = jnp.arange(members, dtype=jnp.int32)
    matches = local_target[:, None] == slot_index[None, :]
    source = jnp.sum(jnp.where(matches, slot_index[:, None], 0), axis=0)
    useful = (base + slot_index)[:, None] >= CHILD_PANELS
    kept_mask = jnp.sum(jnp.where(matches & useful, 1.0, 0.0), axis=0)
    return (source, kept_mask)


def extend_frame(finished, target_map, row_start, col_start):
    height, breadth = finished.shape
    row_blocks = height // BLOCK
    col_blocks = breadth // BLOCK
    row_base = row_start // BLOCK
    col_base = col_start // BLOCK
    row_targets = lax.dynamic_slice_in_dim(target_map, row_base, row_blocks)
    col_targets = lax.dynamic_slice_in_dim(target_map, col_base, col_blocks)
    row_source, row_kept = block_inverse(row_targets, row_base, row_blocks)
    col_source, col_kept = block_inverse(col_targets, col_base, col_blocks)
    tile_grid = finished.reshape(row_blocks, BLOCK, col_blocks, BLOCK)
    tile_grid = jnp.take(tile_grid, row_source, axis=0)
    tile_grid = jnp.take(tile_grid, col_source, axis=2)
    tile_grid = tile_grid * row_kept[:, None, None, None] * col_kept[None, None, :, None]
    return tile_grid.reshape(height, breadth)


def per_device(child_fronts, parent_front, block_maps):
    height = child_fronts.shape[1]
    breadth = child_fronts.shape[2]
    row_start = lax.axis_index("frow") * height
    col_start = lax.axis_index("fcol") * breadth

    def child_diag(column, first_col):
        holder_row = first_col // height
        within = first_col - holder_row * height
        return from_root(column[within : within + BLOCK], "frow", holder_row)

    def child_panel(own_panel, owner_col):
        return from_root(own_panel, "fcol", owner_col)

    def child_columns(framed):
        return lax.psum(framed, "frow")

    finished = factor_panels(
        child_fronts[0], row_start, col_start, CHILD_PANELS, child_diag, child_panel, child_columns
    )
    framed_parent = extend_frame(finished, block_maps[0], row_start, col_start)
    assembled = parent_front + lax.psum(framed_parent, "leaf")

    def parent_diag(column, first_col):
        holder_row = first_col // height
        within = first_col - holder_row * height
        return from_root(column[within : within + BLOCK], "frow", holder_row)

    def parent_panel(own_panel, owner_col):
        return from_root(own_panel, "fcol", owner_col)

    def parent_columns(framed):
        return lax.psum(framed, "frow")

    parent_done = factor_panels(
        assembled, row_start, col_start, PARENT_PANELS, parent_diag, parent_panel, parent_columns
    )
    return (finished[None], parent_done)


def solution(mesh):
    return jax.shard_map(
        per_device,
        mesh=mesh,
        in_specs=(P("leaf", "frow", "fcol"), P("frow", "fcol"), P("leaf", None)),
        out_specs=(P("leaf", "frow", "fcol"), P("frow", "fcol")),
        check_vma=False,
    )
```

profile of v0, /device:TPU:31, one launch (start us, length us, event | category | flops | bytes accessed | tf_op | source)
XLA Modules:
  0.0 615.8 jit_solution(11172521722832910904)
XLA Ops:
  7.2 5.3 copy.49
  12.6 1.5 slice_select_fusion.2
  14.5 31.6 %all-reduce.11.cloned.1.call-done = f32[128,128]{0,1:T(8,128)} async-done(((f32[128,128]{0,1:T(8,128)}), f32[128,128]{0,1:T(8,128)}) %all-reduce.11.cloned.1.call-update) | async-done | bytes 65552 | tf_op jit(solution)/shard_map/psum | solution.py:13
  46.3 11.7 %cholesky.59 = f32[128,128]{1,0:T(8,128)S(1)} custom-call(f32[128,128]{1,0:T(8,128)S(1)} %fusion.22), custom_call_target="Cholesky" | custom-call | tf_op jit(solution)/shard_map/jit(cholesky)/cholesky | solution.py:31
  58.0 0.6 compare_reduce_fusion.2
  58.6 0.7 select_bitcast_fusion.2
  59.3 9.8 %custom-call.7 = f32[1,128,128]{1,2,0:T(8,128)S(1)} custom-call(f32[1,128,128]{2,1,0:T(8,128)S(1)} %get-tuple-element.53), custom_call_target="InvertDiagBlocksLowerTriangular" | custom-call | tf_op jit(solution)/shard_map/triangular_solve/custom-call.0 | solution.py:32
  69.1 2.8 gather_fusion.2
  71.9 0.2 copy.51
  72.1 2.5 fusion.10
  74.8 0.7 compare_reduce_fusion.4
  75.5 34.2 %all-reduce.13.cloned.1.call-done = f32[1024,128]{0,1:T(8,128)} async-done(((f32[1024,128]{0,1:T(8,128)}), f32[1024,128]{0,1:T(8,128)}) %all-reduce.13.cloned.1.call-update) | async-done | bytes 524304 | tf_op jit(solution)/shard_map/psum | solution.py:13
  109.7 1.9 broadcast_select_fusion.2
  111.6 0.2 all-reduce.17.cloned.1.call-start
  111.8 0.1 select_reduce_fusion.3
  111.9 38.7 %all-reduce.15.cloned.1.call-done = f32[1024,128]{0,1:T(8,128)} async-done(((f32[1024,128]{0,1:T(8,128)}), f32[1024,128]{0,1:T(8,128)}) %all-reduce.15.cloned.1.call-update) | async-done | bytes 524304 | tf_op jit(solution)/shard_map/psum | solution.py:96
  150.6 7.0 %and_select_fusion.3 = f32[1024,1024]{0,1:T(8,128)S(1)} fusion(f32[1024,128]{0,1:T(8,128)} %all-reduce.13.cloned.1.call-done, f32[1024,128]{0,1:T(8,128)} %all-reduce.15.cloned.1.call-done, pred[1024]{0:T(1024)(128)(4,1)S(1)} %get-tuple-element.66, pred[1024]{0:T(1024)(128)(4,1)S(1)} %get-tuple-element.65, pred[1024]{0:T(1024)(128)(4,1)S(1)} %fusion.25, ...), kind=kOutput, calls=%fused_computation.8 | convolution fusion | flops 1615855616 | bytes 9440256 | tf_op jit(solution)/shard_map/dot_general | solution.py:44
  157.6 0.8 fusion.11
  158.4 2.0 copy-done.1
  160.4 0.6 slice_select_fusion.1
  161.2 33.3 %all-reduce.17.cloned.1.call-done = f32[128,128]{0,1:T(8,128)} async-done(((f32[128,128]{0,1:T(8,128)}), f32[128,128]{0,1:T(8,128)}) %all-reduce.17.cloned.1.call-update) | async-done | bytes 65552 | tf_op jit(solution)/shard_map/psum | solution.py:13
  194.6 11.7 %cholesky.70 = f32[128,128]{1,0:T(8,128)S(1)} custom-call(f32[128,128]{1,0:T(8,128)S(1)} %fusion.20), custom_call_target="Cholesky" | custom-call | tf_op jit(solution)/shard_map/jit(cholesky)/cholesky | solution.py:31
  206.4 0.6 compare_reduce_fusion.1
  207.0 0.7 select_bitcast_fusion.1
  207.7 9.8 %custom-call.8 = f32[1,128,128]{1,2,0:T(8,128)S(1)} custom-call(f32[1,128,128]{2,1,0:T(8,128)S(1)} %get-tuple-element.51), custom_call_target="InvertDiagBlocksLowerTriangular" | custom-call | tf_op jit(solution)/shard_map/triangular_solve/custom-call.0 | solution.py:32
  217.5 2.8 gather_fusion.3
  220.3 0.2 copy.54
  220.5 2.5 fusion.7
  223.2 0.7 compare_reduce_fusion.3
  223.9 34.1 %all-reduce.19.cloned.1.call-done = f32[1024,128]{0,1:T(8,128)} async-done(((f32[1024,128]{0,1:T(8,128)}), f32[1024,128]{0,1:T(8,128)}) %all-reduce.19.cloned.1.call-update) | async-done | bytes 524304 | tf_op jit(solution)/shard_map/psum | solution.py:13
  258.1 1.9 broadcast_select_fusion.1
  260.0 0.3 all-reduce.23.cloned.1.call-start
  260.4 38.3 %all-reduce.21.cloned.1.call-done = f32[1024,128]{0,1:T(8,128)} async-done(((f32[1024,128]{0,1:T(8,128)}), f32[1024,128]{0,1:T(8,128)}) %all-reduce.21.cloned.1.call-update) | async-done | bytes 524304 | tf_op jit(solution)/shard_map/psum | solution.py:96
  298.7 6.8 %select_select_fusion = f32[1024,1024]{0,1:T(8,128)S(1)} fusion(f32[1024,1024]{0,1:T(8,128)} %copy-done.1, f32[1024,128]{0,1:T(8,128)} %all-reduce.19.cloned.1.call-done, f32[1024,128]{0,1:T(8,128)} %all-reduce.21.cloned.1.call-done, pred[1024]{0:T(1024)(128)(4,1)S(1)} %get-tuple-element.68, pred[1024]{0:T(1024)(128)(4,1)S(1)} %get-tuple-element.67, ...), kind=kOutput, calls=%fused_computation.12 | convolution fusion | flops 1615855616 | bytes 9440256 | tf_op jit(solution)/shard_map/dot_general | solution.py:44
  305.6 0.8 fusion.12
  306.4 3.4 copy.68
  309.8 5.3 copy.56
  315.1 5.0 gather_fusion
  320.1 2.6 broadcast_select_fusion
  322.7 2.8 copy.57
  325.4 4.9 gather_fusion.1
  330.4 5.3 copy.58
  335.7 5.3 fusion.1
  341.0 5.3 copy.59
  346.4 104.0 %all-reduce.23.cloned.1.call-done = f32[1024,1024]{0,1:T(8,128)} async-done(((f32[1024,1024]{0,1:T(8,128)}), f32[1024,1024]{0,1:T(8,128)}) %all-reduce.23.cloned.1.call-update) | async-done | bytes 4194320 | tf_op jit(solution)/shard_map/psum | solution.py:102
  450.3 4.4 add.160
  454.7 1.9 copy-done.2
  456.7 0.6 slice_select_fusion
  457.3 0.3 all-reduce.27.cloned.1.call-start
  457.6 31.7 %all-reduce.25.cloned.1.call-done = f32[128,128]{0,1:T(8,128)} async-done(((f32[128,128]{0,1:T(8,128)}), f32[128,128]{0,1:T(8,128)}) %all-reduce.25.cloned.1.call-update) | async-done | bytes 65552 | tf_op jit(solution)/shard_map/psum | solution.py:13
  489.5 11.7 %cholesky.81 = f32[128,128]{1,0:T(8,128)S(1)} custom-call(f32[128,128]{1,0:T(8,128)S(1)} %fusion.18), custom_call_target="Cholesky" | custom-call | tf_op jit(solution)/shard_map/jit(cholesky)/cholesky | solution.py:31
  501.3 0.6 compare_reduce_fusion
  501.9 0.7 select_bitcast_fusion
  502.6 9.8 %custom-call.9 = f32[1,128,128]{1,2,0:T(8,128)S(1)} custom-call(f32[1,128,128]{2,1,0:T(8,128)S(1)} %get-tuple-element.49), custom_call_target="InvertDiagBlocksLowerTriangular" | custom-call | tf_op jit(solution)/shard_map/triangular_solve/custom-call.0 | solution.py:32
  512.4 2.8 gather_fusion.4
  515.2 0.2 copy.61
  515.4 2.5 fusion.4
  518.0 34.9 %all-reduce.27.cloned.1.call-done = f32[1024,128]{0,1:T(8,128)} async-done(((f32[1024,128]{0,1:T(8,128)}), f32[1024,128]{0,1:T(8,128)}) %all-reduce.27.cloned.1.call-update) | async-done | bytes 524304 | tf_op jit(solution)/shard_map/psum | solution.py:13
  553.0 1.9 broadcast_select_fusion.3
  554.9 5.4 copy.63
  560.3 32.8 %all-reduce.29.cloned.1.call-done = f32[1024,128]{0,1:T(8,128)} async-done(((f32[1024,128]{0,1:T(8,128)}), f32[1024,128]{0,1:T(8,128)}) %all-reduce.29.cloned.1.call-update) | async-done | bytes 524304 | tf_op jit(solution)/shard_map/psum | solution.py:113
  593.1 7.6 %and_select_fusion.2 = f32[1024,1024]{0,1:T(8,128)} fusion(f32[1024,1024]{0,1:T(8,128)} %copy-done.2, f32[1024,128]{0,1:T(8,128)S(1)} %copy-done.5, f32[1024,128]{0,1:T(8,128)} %all-reduce.29.cloned.1.call-done, pred[1024]{0:T(1024)(128)(4,1)S(1)} %get-tuple-element.66, pred[1024]{0:T(1024)(128)(4,1)S(1)} %get-tuple-element.65, pred[1024]{0:T(1024)(128)(4,1)S(1)} %fusion.25), kind=kOutput, calls=%fused_computation.7 | convolution fusion | flops 1615855616 | bytes 9440256 | tf_op jit(solution)/shard_map/dot_general | solution.py:44
  600.6 2.5 fusion.13
  603.2 5.3 copy.64
  (62 shorter events, 1.6 us)
Async XLA Ops:
  7.2 38.9 %all-reduce.11.cloned.1.call-start = ((), (), s32[]{:S(2)}) async-start(), calls=%async_computation | async-start | bytes 131072 | tf_op jit(solution)/shard_map/psum | solution.py:13
  7.2 7.0 %copy-start.6 = (s32[1,32]{1,0:T(1,128)S(1)}, s32[1,32]{1,0:T(1,128)}, u32[]{:S(2)}) copy-start(s32[1,32]{1,0:T(1,128)} %param.16) | copy-start | bytes 388
  14.1 95.6 %all-reduce.13.cloned.1.call-start = ((), (), s32[]{:S(2)}) async-start(), calls=%async_computation.1 | async-start | bytes 1048576 | tf_op jit(solution)/shard_map/psum | solution.py:13
  74.7 75.9 %all-reduce.15.cloned.1.call-start = ((), (), s32[]{:S(2)}) async-start(), calls=%async_computation.2 | async-start | bytes 1048576 | tf_op jit(solution)/shard_map/psum | solution.py:96
  111.6 82.9 %all-reduce.17.cloned.1.call-start = ((), (), s32[]{:S(2)}) async-start(), calls=%async_computation.3 | async-start | bytes 131072 | tf_op jit(solution)/shard_map/psum | solution.py:13
  150.6 7.0 %copy-start.3 = (f32[1024,128]{0,1:T(8,128)S(1)}, f32[1024,128]{0,1:T(8,128)}, u32[]{:S(2)}) copy-start(f32[1024,128]{0,1:T(8,128)} %all-reduce.13.cloned.1.call-done) | copy-start | bytes 1572868
  158.4 2.0 copy-start.1
  161.1 97.0 %all-reduce.19.cloned.1.call-start = ((), (), s32[]{:S(2)}) async-start(), calls=%async_computation.4 | async-start | bytes 1048576 | tf_op jit(solution)/shard_map/psum | solution.py:13
  223.1 75.6 %all-reduce.21.cloned.1.call-start = ((), (), s32[]{:S(2)}) async-start(), calls=%async_computation.5 | async-start | bytes 1048576 | tf_op jit(solution)/shard_map/psum | solution.py:96
  260.0 190.4 %all-reduce.23.cloned.1.call-start = ((), (), s32[]{:S(2)}) async-start(), calls=%async_computation.6 | async-start | bytes 8388608 | tf_op jit(solution)/shard_map/psum | solution.py:102
  298.7 6.8 %copy-start.4 = (f32[1024,128]{0,1:T(8,128)S(1)}, f32[1024,128]{0,1:T(8,128)}, u32[]{:S(2)}) copy-start(f32[1024,128]{0,1:T(8,128)} %all-reduce.19.cloned.1.call-done) | copy-start | bytes 1572868
  306.4 3.4 copy-start
  341.0 148.4 %all-reduce.25.cloned.1.call-start = ((), (), s32[]{:S(2)}) async-start(), calls=%async_computation.7 | async-start | bytes 131072 | tf_op jit(solution)/shard_map/psum | solution.py:13
  454.7 1.9 copy-start.2
  457.3 95.6 %all-reduce.27.cloned.1.call-start = ((), (), s32[]{:S(2)}) async-start(), calls=%async_computation.8 | async-start | bytes 1048576 | tf_op jit(solution)/shard_map/psum | solution.py:13
  518.0 75.1 %all-reduce.29.cloned.1.call-start = ((), (), s32[]{:S(2)}) async-start(), calls=%async_computation.9 | async-start | bytes 1048576 | tf_op jit(solution)/shard_map/psum | solution.py:113
  554.9 38.2 %copy-start.5 = (f32[1024,128]{0,1:T(8,128)S(1)}, f32[1024,128]{0,1:T(8,128)}, u32[]{:S(2)}) copy-start(f32[1024,128]{0,1:T(8,128)} %all-reduce.27.cloned.1.call-done) | copy-start | bytes 1572868
Sparse Core Ops, SparseCore 0:
  14.2 31.8 all-reduce.10
  74.8 34.8 all-reduce.12
  112.7 37.8 all-reduce.14
  161.2 33.2 all-reduce.16
  223.2 34.8 all-reduce.18
  260.9 37.8 all-reduce.20
  341.1 109.1 all-reduce.22
  457.4 31.8 all-reduce.24
  518.1 34.8 all-reduce.26
  555.2 37.8 all-reduce.28
where the time goes:
time: 627 us; the launch traced here: 616 us
  waiting for transfers between devices  414 us (66%)
  other arithmetic  95.4 us (15%)
  local copies, waits for them, and re-layouts  61.6 us (10%)
  matrix products  29 us (5%)
  between operations  15.1 us (2%)
    psum x6, waiting for transfers between devices, from_root(): return lax.psum(jnp.where(mine, shard, jnp.zeros_like(shard)), axis)  200 us
    psum x1, waiting for transfers between devices, per_device(): assembled = parent_front + lax.psum(framed_parent, 'leaf')  104 us
    psum x2, waiting for transfers between devices, child_columns(): return lax.psum(framed, 'frow')  77 us
    another operation x9, other arithmetic, factor_panels(): factor = jnp.linalg.cholesky(pivot_block)  37.2 us
    psum x1, waiting for transfers between devices, parent_columns(): return lax.psum(framed, 'frow')  32.8 us
    another operation x6, other arithmetic, factor_panels(): lax.linalg.triangular_solve(factor, column, left_side=False, lower=True,...  31.4 us
    unnamed x19, local copies, waits for them, and re-layouts  28.8 us
    dot_general x3, matrix products, factor_panels(): update = jnp.dot(shared, across.T, precision=lax.Precision.HIGHEST)  21.4 us
  transfers between devices with their start and end apart: 10, of which 10 were waited for; matrix products, arithmetic and copies ran while one was open for 2% of the time, Pallas kernels for 0%

commit v1 on v0

v1 whole, which is shorter than its diff:
```python
import functools

import jax
import jax.numpy as jnp
from jax import lax
from jax.experimental import pallas as pl
from jax.experimental.pallas import tpu as pltpu
from jax.sharding import PartitionSpec as P

BLOCK = 128
CHILD_PANELS = 2
WIDE = BLOCK * CHILD_PANELS
HIGHEST = lax.Precision.HIGHEST


def dot(a, b, contract=((1,), (0,))):
    return lax.dot_general(
        a, b, (contract, ((), ())), precision=HIGHEST, preferred_element_type=jnp.float32
    )


def factor_block(matrix):
    groups = BLOCK // 8
    sub = lax.broadcasted_iota(jnp.int32, (8, BLOCK), 0)
    lane = lax.broadcasted_iota(jnp.int32, (8, BLOCK), 1)
    rows = [matrix[g * 8 : g * 8 + 8, :] for g in range(groups)]
    inverse = [jnp.where(lane == sub + g * 8, 1.0, 0.0) for g in range(groups)]
    for k in range(BLOCK):
        own, within = divmod(k, 8)
        pivot_row = rows[own][within : within + 1, :]
        scale = 1.0 / pivot_row[:, k : k + 1]
        pivot_row = pivot_row * scale
        inverse_row = inverse[own][within : within + 1, :] * scale
        for g in range(own, groups):
            if g == own and within == 7:
                continue
            column = rows[g][:, k : k + 1]
            if g == own:
                column = jnp.where(sub[:, :1] > within, column, 0.0)
            rows[g] = rows[g] - column * pivot_row
            inverse[g] = inverse[g] - column * inverse_row
    upper, lower_inverse = [], []
    for g in range(groups):
        diagonal = jnp.sum(jnp.where(lane == sub + g * 8, rows[g], 0.0), axis=1, keepdims=True)
        root = 1.0 / jnp.sqrt(diagonal)
        upper.append(jnp.where(lane >= sub + g * 8, rows[g] * root, 0.0))
        lower_inverse.append(inverse[g] * root)
    return jnp.concatenate(upper, axis=0), jnp.concatenate(lower_inverse, axis=0)


def factor_kernel(panels, d_ref, k_ref, w_ref):
    k_ref[...] = jnp.zeros_like(k_ref)
    w_ref[...] = jnp.zeros_like(w_ref)
    for p in range(panels):
        c = slice(p * BLOCK, (p + 1) * BLOCK)
        block = d_ref[c, c]
        if p:
            before = slice(0, p * BLOCK)
            left = dot(d_ref[c, before], w_ref[before, before], ((1,), (1,)))
            k_ref[c, before] = left
            block = block - dot(left, left, ((1,), (1,)))
        upper, inverse = factor_block(block)
        k_ref[c, c] = upper.T
        w_ref[c, c] = inverse
        if p:
            w_ref[c, before] = -dot(inverse, dot(left, w_ref[before, before]))


def factor(pivot):
    size = pivot.shape[0]
    shape = jax.ShapeDtypeStruct((size, size), jnp.float32)
    return pl.pallas_call(
        functools.partial(factor_kernel, size // BLOCK),
        out_shape=(shape, shape),
        in_specs=[pl.BlockSpec(memory_space=pltpu.VMEM)],
        out_specs=(pl.BlockSpec(memory_space=pltpu.VMEM),) * 2,
        cost_estimate=pl.CostEstimate(
            flops=size * BLOCK * 2000, bytes_accessed=3 * size * size * 4, transcendentals=0
        ),
        name="factor_pivot",
    )(pivot)


def parent_kernel(children, tables, where_am_i, *refs):
    front, panel_rows, panel_cols, pivot_factor = refs[:4]
    blocks = refs[4 : 4 + children]
    left = refs[4 + children : 4 + 2 * children]
    right = refs[4 + 2 * children : 4 + 3 * children]
    out, held = refs[4 + 3 * children], refs[5 + 3 * children]
    r = pl.program_id(0)
    row_blocks = pl.num_programs(0)
    col_blocks = out.shape[1] // BLOCK
    for s in range(children):
        held[s] = blocks[s][...] - dot(left[s][...], right[s][...])
    update = dot(panel_rows[...], panel_cols[...])
    first_row = (where_am_i[0] == 0) & (r == 0)
    for c in range(col_blocks):
        cols = slice(c * BLOCK, (c + 1) * BLOCK)
        tile = front[:, cols]
        for s in range(children):
            source = tables[s, 2, c]
            keep = tables[s, 1, r] * tables[s, 3, c]
            piece = held[s, :, pl.ds(pl.multiple_of(source * BLOCK, BLOCK), BLOCK)]
            tile = tile + jnp.where(keep > 0, piece, 0.0)
        tile = tile - update[:, cols]
        tile = jnp.where(first_row, 0.0, tile)
        if c == 0:
            pivot = jnp.where(first_row, pivot_factor[...], panel_rows[...])
            tile = jnp.where(where_am_i[1] == 0, pivot, tile)
        out[:, cols] = tile


def finish_parent(tables, where_am_i, front, panel_rows, panel_cols, pivot_factor, blocks, left, right):
    height, breadth = front.shape
    children = len(blocks)

    def moved(s):
        return lambda r, tables, where_am_i: (tables[s, 0, r], 0)

    def row(r, tables, where_am_i):
        return (r, 0)

    def whole(r, tables, where_am_i):
        return (0, 0)

    return pl.pallas_call(
        functools.partial(parent_kernel, children),
        grid_spec=pltpu.PrefetchScalarGridSpec(
            num_scalar_prefetch=2,
            grid=(height // BLOCK,),
            in_specs=[
                pl.BlockSpec((BLOCK, breadth), row),
                pl.BlockSpec((BLOCK, BLOCK), row),
                pl.BlockSpec((BLOCK, breadth), whole),
                pl.BlockSpec((BLOCK, BLOCK), whole),
            ]
            + [pl.BlockSpec((BLOCK, breadth), moved(s)) for s in range(children)]
            + [pl.BlockSpec((BLOCK, WIDE), moved(s)) for s in range(children)]
            + [pl.BlockSpec((WIDE, breadth), whole) for s in range(children)],
            out_specs=pl.BlockSpec((BLOCK, breadth), row),
            scratch_shapes=[pltpu.VMEM((children, BLOCK, breadth), jnp.float32)],
        ),
        out_shape=jax.ShapeDtypeStruct((height, breadth), jnp.float32),
        compiler_params=pltpu.CompilerParams(
            dimension_semantics=("arbitrary",), vmem_limit_bytes=40 * 2**20
        ),
        cost_estimate=pl.CostEstimate(
            flops=2 * height * breadth * (WIDE * children + BLOCK) * 6,
            bytes_accessed=height * breadth * 4 * (children + 2),
            transcendentals=0,
        ),
        name="finish_parent",
    )(tables, where_am_i, front, panel_rows, panel_cols, pivot_factor, *blocks, *left, *right)


def moved_blocks(array, source, kept, axis):
    pieces = []
    for place in range(array.shape[axis] // BLOCK):
        piece = lax.dynamic_slice_in_dim(array, source[place] * BLOCK, BLOCK, axis)
        pieces.append(jnp.where(kept[place] > 0, piece, 0.0))
    return jnp.concatenate(pieces, axis)


def per_device(leaves, frows, fcols, child_fronts, parent_front, block_maps):
    own = child_fronts[0]
    height, breadth = own.shape
    row_blocks, col_blocks = height // BLOCK, breadth // BLOCK
    l, i, j = lax.axis_index("leaf"), lax.axis_index("frow"), lax.axis_index("fcol")
    axes = ("leaf", "frow", "fcol")

    def send(x, moves):
        flat = lambda c: (c[0] * frows + c[1]) * fcols + c[2]
        return lax.ppermute(x, axes, [(flat(a), flat(b)) for a, b in moves])

    def along_row(x):
        step = fcols // 2
        while step:
            sources = range(0, fcols, 2 * step)
            moves = [
                ((a, b, c), (a, b, c + step))
                for a in range(leaves) for b in range(frows) for c in sources
            ]
            x = jnp.where(lax.rem(j, 2 * step) == step, send(x, moves), x)
            step //= 2
        return x

    def along_col(x, columns):
        for b in range(frows - 1):
            moves = [((a, b, c), (a, b + 1, c)) for a in range(leaves) for c in columns]
            x = jnp.where(i == b + 1, send(x, moves), x)
        return x

    def from_leaf(x, shift, rows=range(frows), columns=range(fcols)):
        return send(
            x,
            [((a, b, c), ((a + shift) % leaves, b, c)) for a in range(leaves) for b in rows for c in columns],
        )

    number = jnp.arange(block_maps.shape[1], dtype=jnp.int32)
    maps = [block_maps[0]] + [lax.ppermute(block_maps[0], "leaf", [(a, (a + s) % leaves) for a in range(leaves)]) for s in range(1, leaves)]
    inverses = [jnp.sum(jnp.where(m[:, None] == number[None, :], number[:, None], 0), axis=0) for m in maps]
    width = max(row_blocks, col_blocks)
    tables = []
    for inverse in inverses:
        mine_rows = lax.dynamic_slice_in_dim(inverse, i * row_blocks, row_blocks)
        mine_cols = lax.dynamic_slice_in_dim(inverse, j * col_blocks, col_blocks)
        lines = [
            mine_rows - i * row_blocks,
            (mine_rows >= CHILD_PANELS).astype(jnp.int32),
            mine_cols - j * col_blocks,
            (mine_cols >= CHILD_PANELS).astype(jnp.int32),
        ]
        tables.append(jnp.stack([jnp.pad(line, (0, width - line.shape[0])) for line in lines]))
    tables = jnp.stack(tables)
    first = [inverse[0] for inverse in inverses]

    own_rows = jnp.concatenate(
        [own[:, :WIDE], lax.dynamic_slice(own, (0, first[0] * BLOCK), (height, BLOCK))], axis=1
    )
    own_cols = jnp.concatenate(
        [own[:WIDE], lax.dynamic_slice(own, (first[0] * BLOCK, 0), (BLOCK, breadth))], axis=0
    )
    raw_rows = [own_rows] + [from_leaf(own_rows, s, columns=(0,)) for s in range(1, leaves)]
    raw_cols = [own_cols] + [from_leaf(own_cols, s, rows=(0,)) for s in range(1, leaves)]
    blocks = [own] + [from_leaf(own, s) for s in range(1, leaves)]

    left, right, factors = [], [], []
    for s in range(leaves):
        pivot = along_col(raw_rows[s][:WIDE, :WIDE], (0,))
        message = along_row(jnp.concatenate([pivot, raw_rows[s][:, :WIDE]], axis=0))
        cols = along_col(raw_cols[s][:WIDE], range(fcols))
        k, w = factor(message[:WIDE])
        factors.append(k)
        left.append(dot(message[WIDE:], w, ((1,), (1,))))
        right.append(dot(w, cols))

    global_rows = i * height + jnp.arange(height, dtype=jnp.int32)[:, None]
    global_cols = j * breadth + jnp.arange(breadth, dtype=jnp.int32)[None, :]
    trailing = (global_rows >= WIDE) & (global_cols >= WIDE)
    finished = jnp.where(trailing, own - dot(left[0], right[0]), 0.0)
    panel = jnp.concatenate([jnp.where(i == 0, factors[0], left[0][:WIDE]), left[0][WIDE:]], axis=0)
    finished = finished.at[:, :WIDE].set(jnp.where(j == 0, panel, finished[:, :WIDE]))

    panel_rows, panel_cols = parent_front[:, :BLOCK], parent_front[:BLOCK]
    for s in range(leaves):
        across = lax.dynamic_slice(right[s], (0, first[s] * BLOCK), (WIDE, BLOCK))
        part = raw_rows[s][:, WIDE:] - dot(left[s], across)
        part = moved_blocks(part, tables[s, 0], tables[s, 1], 0)
        panel_rows = panel_rows + jnp.where(first[s] >= CHILD_PANELS, part, 0.0)
        down = lax.dynamic_slice(left[s], (first[s] * BLOCK, 0), (BLOCK, WIDE))
        part = raw_cols[s][WIDE:] - dot(down, right[s])
        part = moved_blocks(part, tables[s, 2], tables[s, 3], 1)
        panel_cols = panel_cols + jnp.where(first[s] >= CHILD_PANELS, part, 0.0)
    pivot = along_col(panel_rows[:BLOCK], (0,))
    message = along_row(jnp.concatenate([pivot, panel_rows], axis=0))
    panel_cols = along_col(panel_cols, range(fcols))
    k, w = factor(message[:BLOCK])
    panel_rows = dot(message[BLOCK:], w, ((1,), (1,)))
    panel_cols = dot(w, panel_cols)

    where_am_i = jnp.stack([i, j]).astype(jnp.int32)
    parent = finish_parent(
        tables, where_am_i, parent_front, panel_rows, panel_cols, k, blocks, left, right
    )
    return (finished[None], parent)


def solution(mesh):
    return jax.shard_map(
        functools.partial(per_device, mesh.shape["leaf"], mesh.shape["frow"], mesh.shape["fcol"]),
        mesh=mesh,
        in_specs=(P("leaf", "frow", "fcol"), P("frow", "fcol"), P("leaf", None)),
        out_specs=(P("leaf", "frow", "fcol"), P("frow", "fcol")),
        check_vma=False,
    )
```

time: 627 us -> 336 us (0.54)
  the two profiles are of different devices: /device:TPU:31 before, /device:TPU:16 now
where the time goes in v1:
time: 336 us; the launch traced here: 330 us
  waiting for transfers between devices  91.5 us (27%)
  Pallas kernels  75.7 us (23%)
  starting transfers between devices  47.7 us (14%)
  between operations  42.5 us (13%)
  matrix products  25.2 us (8%)
  local copies, waits for them, and re-layouts  24.9 us (7%)
  other arithmetic  22.5 us (7%)
    ppermute x1, waiting for transfers between devices, per_device(): lax.ppermute(block_maps[0], 'leaf', [(a, (a + s) % leaves) for a in range...  65.1 us
    pallas_call x3, Pallas kernels, factor(): pl.pallas_call(functools.partial(factor_kernel, size // BLOCK), out_shape...  60.2 us
    ppermute x27, starting transfers between devices, send(): return lax.ppermute(x, axes, [(flat(a), flat(b)) for a, b in moves])  47.2 us
    ppermute x27, waiting for transfers between devices, send(): return lax.ppermute(x, axes, [(flat(a), flat(b)) for a, b in moves])  26.4 us
    dot_general x11, matrix products, dot(): lax.dot_general(a, b, (contract, ((), ())), precision=HIGHEST, preferred_...  25.2 us
    pallas_call x1, Pallas kernels, finish_parent(): pl.pallas_call(functools.partial(parent_kernel, children), grid_spec=pltp...  15.5 us
    select_n x15, other arithmetic, along_col(): x = jnp.where(i == b + 1, send(x, moves), x)  10.4 us
    unnamed x47, local copies, waits for them, and re-layouts  9.61 us
  transfers between devices with their start and end apart: 28, of which 7 were waited for; matrix products, arithmetic and copies ran while one was open for 19% of the time, Pallas kernels for 18%

profile of v1, /device:TPU:16, one launch (start us, length us, event | category | flops | bytes accessed | tf_op | source)
XLA Modules:
  0.0 330.0 jit_solution(12587532000448592093)
XLA Ops:
  0.6 1.6 collective-permute-start.27
  3.9 2.3 slice_bitcast_fusion
  6.2 1.6 collective-permute-start.5
  8.3 1.3 slice.503
  9.8 1.1 dynamic-slice_bitcast_fusion.1
  10.9 1.2 pad_maximum_fusion
  12.1 3.4 %collective-permute-start.9 = (f32[1024,384]{1,0:T(8,128)}, f32[1024,384]{1,0:T(8,128)}, u32[]{:S(2)}, u32[]{:S(2)}) collective-permute-start(f32[1024,384]{1,0:T(8,128)} %pad_maximum_fusion), channel_id=1, source_target_pairs={{0,16},{4,20},{8,24},{12,28},{16,0},{20,4},{24,8},{28,12}} | collective-permute-start | bytes 4718600 | tf_op jit(solution)/shard_map/ppermute | solution.py:173
  15.7 1.1 dynamic-slice_bitcast_fusion
  17.8 1.3 collective-permute-start.1
  19.1 2.5 pad_maximum_fusion.1
  21.7 4.4 %collective-permute-done.1 = f32[256,256]{1,0:T(8,128)S(1)} collective-permute-done((f32[256,256]{1,0:T(8,128)S(1)}, f32[256,256]{1,0:T(8,128)S(1)}, u32[]{:S(2)}, u32[]{:S(2)}) %collective-permute-start.1) | collective-permute-done | bytes 262176 | tf_op jit(solution)/shard_map/ppermute | solution.py:173
  26.1 1.3 collective-permute-start.2
  28.3 65.1 %collective-permute-done.8 = s32[32]{0:T(128)S(1)} collective-permute-done((s32[32]{0:T(128)S(1)}, s32[32]{0:T(128)S(1)}, u32[]{:S(2)}, u32[]{:S(2)}) %collective-permute-start.8) | collective-permute-done | bytes 160 | tf_op jit(solution)/shard_map/ppermute | solution.py:200
  94.3 1.1 pad_maximum_fusion.2
  95.4 4.5 %collective-permute-start.3 = (f32[1280,256]{1,0:T(8,128)}, f32[1280,256]{1,0:T(8,128)}, u32[]{:S(2)}, u32[]{:S(2)}) collective-permute-start(f32[1280,256]{1,0:T(8,128)} %pad_maximum_fusion.2), channel_id=1, source_target_pairs={{0,2},{4,6},{8,10},{12,14},{16,18},{20,22},{24,26},{28,30}} | collective-permute-start | bytes 3932168 | tf_op jit(solution)/shard_map/ppermute | solution.py:173
  120.6 1.7 slice.510
  122.3 1.4 collective-permute-start.10
  123.7 2.4 broadcast_select_fusion.5
  126.0 1.3 collective-permute-start.6
  151.9 1.3 slice.511
  154.2 1.3 collective-permute-start.11
  155.7 1.4 collective-permute-start.4
  157.1 7.0 %collective-permute-done.11 = f32[256,256]{1,0:T(8,128)S(1)} collective-permute-done((f32[256,256]{1,0:T(8,128)S(1)}, f32[256,256]{1,0:T(8,128)S(1)}, u32[]{:S(2)}, u32[]{:S(2)}) %collective-permute-start.11) | collective-permute-done | bytes 262176 | tf_op jit(solution)/shard_map/ppermute | solution.py:173
  164.1 1.3 collective-permute-start.12
  165.5 1.4 broadcast_select_fusion.7
  166.9 2.6 collective-permute-start.7
  169.5 2.7 collective-permute-done.12
  172.2 1.1 pad_maximum_fusion.3
  173.4 2.4 collective-permute-start.13
  175.8 1.1 broadcast_select_fusion.4
  176.9 1.8 collective-permute-start.17
  178.9 1.0 copy-done.9
  180.7 24.0 %factor_pivot.3 = (f32[256,256]{1,0:T(8,128)}, f32[256,256]{1,0:T(8,128)}) custom-call(f32[256,256]{1,0:T(8,128)} %slice.505.d_ref), custom_call_target="tpu_custom_call" | custom-call | flops 65536000 | bytes 786432 | tf_op jit(solution)/shard_map/factor_pivot/pallas_call | solution.py:72
  204.7 2.3 fusion.4.refs_6_
  207.1 2.6 fusion.8.refs_8_
  209.7 1.8 convolution_subtract_fusion
  211.7 2.0 convolution_subtract_fusion.1
  214.1 1.4 collective-permute-start.14
  215.7 2.4 broadcast_select_fusion.6
  218.1 5.7 %collective-permute-start.18 = (f32[256,1024]{1,0:T(8,128)}, f32[256,1024]{1,0:T(8,128)}, u32[]{:S(2)}, u32[]{:S(2)}) collective-permute-start(f32[256,1024]{1,0:T(8,128)} %broadcast_select_fusion.6), channel_id=1, source_target_pairs={{8,12},{9,13},{10,14},{11,15},{24,28},{25,29},{26,30},{27,31}} | collective-permute-start | bytes 3145736 | tf_op jit(solution)/shard_map/ppermute | solution.py:173
  224.6 1.1 copy-done.8
  226.4 24.0 %factor_pivot.4 = (f32[256,256]{1,0:T(8,128)}, f32[256,256]{1,0:T(8,128)}) custom-call(f32[256,256]{1,0:T(8,128)} %slice.513.d_ref), custom_call_target="tpu_custom_call" | custom-call | flops 65536000 | bytes 786432 | tf_op jit(solution)/shard_map/factor_pivot/pallas_call | solution.py:72
  250.4 2.3 fusion.2.refs_7_
  252.7 2.3 fusion.6.refs_9_
  255.0 2.4 slice_subtract_fusion.1
  257.7 1.1 select_add_fusion.1
  259.8 1.8 slice_subtract_fusion
  261.9 1.6 collective-permute-start.20
  263.4 4.8 %collective-permute-done.20 = f32[128,128]{1,0:T(8,128)S(1)} collective-permute-done((f32[128,128]{1,0:T(8,128)S(1)}, f32[128,128]{1,0:T(8,128)S(1)}, u32[]{:S(2)}, u32[]{:S(2)}) %collective-permute-start.20) | collective-permute-done | bytes 65568 | tf_op jit(solution)/shard_map/ppermute | solution.py:173
  268.3 1.3 collective-permute-start.21
  269.6 1.2 select_add_fusion
  271.6 1.3 collective-permute-start.22
  272.9 4.2 %subtract_select_fusion = f32[1024,1024]{1,0:T(8,128)S(1)} fusion(f32[1024,256]{1,0:T(8,128)S(1)} %fusion.4.refs_6_, f32[256,1024]{1,0:T(8,128)S(1)} %fusion.8.refs_8_, pred[1024]{0:T(1024)(128)(4,1)S(1)} %add_compare_fusion, pred[1024]{0:T(1024)(128)(4,1)S(1)} %add_compare_fusion.1, f32[1,1024,1024]{2,1,0:T(8,128)S(1)} %copy-done), kind=kOutput, calls=%fused_computation | convolution fusion | flops 3224371200 | bytes 10487808 | tf_op jit(solution)/shard_map/dot_general | solution.py:17
  277.2 1.3 collective-permute-start.25
  278.5 1.7 collective-permute-done.22
  280.3 1.3 collective-permute-start.23
  283.7 5.7 %collective-permute-done.25 = f32[128,1024]{1,0:T(8,128)S(1)} collective-permute-done((f32[128,1024]{1,0:T(8,128)S(1)}, f32[128,1024]{1,0:T(8,128)S(1)}, u32[]{:S(2)}, u32[]{:S(2)}) %collective-permute-start.25) | collective-permute-done | bytes 524320 | tf_op jit(solution)/shard_map/ppermute | solution.py:173
  290.3 2.3 collective-permute-start.26
  294.1 12.3 %factor_pivot.5 = (f32[128,128]{1,0:T(8,128)}, f32[128,128]{1,0:T(8,128)}) custom-call(f32[128,128]{1,0:T(8,128)} %slice.517.d_ref), custom_call_target="tpu_custom_call" | custom-call | flops 32768000 | bytes 196608 | tf_op jit(solution)/shard_map/factor_pivot/pallas_call | solution.py:72
  306.4 1.7 fusion.10.refs_1_
  308.1 1.7 fusion.12.refs_2_
  309.9 2.2 copy-done.1
  312.1 2.2 copy-done.6
  314.3 15.5 %finish_parent.1 = f32[1024,1024]{1,0:T(8,128)} custom-call(s32[2,4,8]{2,1,0:T(4,128)S(1)} %pad_add_fusion.tables, s32[2]{0:T(128)S(1)} %pad_add_fusion.1.where_am_i, f32[1024,1024]{1,0:T(8,128)S(1)} %copy-done.6, f32[1024,128]{1,0:T(8,128)S(1)} %fusion.10.refs_1_, f32[128,1024]{1,0:T(8,128)S(1)} %fusion.12.refs_2_, f32[128,128]{1,0:T(8,128)S(1)} %copy-done.7, ...), custom_call_target="tpu_custom_call" | custom-call | flops 8053063680 | bytes 16777216 | tf_op jit(solution)/shard_map/finish_parent/pallas_call | solution.py:126
  (146 shorter events, 21.0 us)
Async XLA Ops:
  0.6 7.2 %copy-start.22 = (s32[1,32]{1,0:T(1,128)S(1)}, s32[1,32]{1,0:T(1,128)}, u32[]{:S(2)}) copy-start(s32[1,32]{1,0:T(1,128)} %param.7) | copy-start | bytes 388
  0.6 309.2 %collective-permute-start.27 = (f32[1024,1024]{1,0:T(8,128)}, f32[1024,1024]{1,0:T(8,128)}, u32[]{:S(2)}, u32[]{:S(2)}) collective-permute-start(f32[1024,1024]{1,0:T(8,128)} %bitcast.124), channel_id=1, source_target_pairs={{0,16},{1,17},{2,18},{3,19},{4,20},{5,21},{6,22},{7,23},{8,24},{9,... | collective-permute-start | bytes 12582920 | tf_op jit(solution)/shard_map/ppermute | solution.py:173
  3.2 13.6 %collective-permute-start = (f32[256,256]{1,0:T(8,128)S(1)}, f32[256,256]{1,0:T(8,128)S(1)}, u32[]{:S(2)}, u32[]{:S(2)}) collective-permute-start(f32[256,256]{1,0:T(8,128)S(1)} %slice.502), channel_id=1, source_target_pairs={{0,4},{16,20}} | collective-permute-start | bytes 786440 | tf_op jit(solution)/shard_map/ppermute | solution.py:173
  6.2 117.4 %collective-permute-start.5 = (f32[256,1024]{1,0:T(8,128)}, f32[256,1024]{1,0:T(8,128)}, u32[]{:S(2)}, u32[]{:S(2)}) collective-permute-start(f32[256,1024]{1,0:T(8,128)} %slice_bitcast_fusion), channel_id=1, source_target_pairs={{0,4},{1,5},{2,6},{3,7},{16,20},{17,21},{18,22},{19,23}} | collective-permute-start | bytes 3145736 | tf_op jit(solution)/shard_map/ppermute | solution.py:173
  7.8 85.5 %collective-permute-start.8 = (s32[32]{0:T(128)S(1)}, s32[32]{0:T(128)S(1)}, u32[]{:S(2)}, u32[]{:S(2)}) collective-permute-start(s32[32]{0:T(128)S(1)} %bitcast.134), channel_id=1, source_target_pairs={{0,16},{16,0},{1,17},{17,1},{2,18},{18,2},{3,19},{19,3},{4,20},{20... | collective-permute-start | bytes 392 | tf_op jit(solution)/shard_map/ppermute | solution.py:200
  12.1 108.5 %collective-permute-start.9 = (f32[1024,384]{1,0:T(8,128)}, f32[1024,384]{1,0:T(8,128)}, u32[]{:S(2)}, u32[]{:S(2)}) collective-permute-start(f32[1024,384]{1,0:T(8,128)} %pad_maximum_fusion), channel_id=1, source_target_pairs={{0,16},{4,20},{8,24},{12,28},{16,0},{20,4},{24,8},{28,12}} | collective-permute-start | bytes 4718600 | tf_op jit(solution)/shard_map/ppermute | solution.py:173
  17.8 8.3 %collective-permute-start.1 = (f32[256,256]{1,0:T(8,128)S(1)}, f32[256,256]{1,0:T(8,128)S(1)}, u32[]{:S(2)}, u32[]{:S(2)}) collective-permute-start(f32[256,256]{1,0:T(8,128)S(1)} %broadcast_select_fusion.13), channel_id=1, source_target_pairs={{4,8},{20,24}} | collective-permute-start | bytes 786440 | tf_op jit(solution)/shard_map/ppermute | solution.py:173
  26.1 68.1 %collective-permute-start.2 = (f32[256,256]{1,0:T(8,128)S(1)}, f32[256,256]{1,0:T(8,128)S(1)}, u32[]{:S(2)}, u32[]{:S(2)}) collective-permute-start(f32[256,256]{1,0:T(8,128)S(1)} %broadcast_select_fusion.15), channel_id=1, source_target_pairs={{8,12},{24,28}} | collective-permute-start | bytes 786440 | tf_op jit(solution)/shard_map/ppermute | solution.py:173
  93.3 56.7 %collective-permute-start.15 = (f32[384,1024]{1,0:T(8,128)}, f32[384,1024]{1,0:T(8,128)S(1)}, u32[]{:S(2)}, u32[]{:S(2)}) collective-permute-start(f32[384,1024]{1,0:T(8,128)} %pad_maximum_fusion.1), channel_id=1, source_target_pairs={{0,16},{1,17},{2,18},{3,19},{16,0},{17,1},{18,2},{19,3}} | collective-permute-start | bytes 4718600 | tf_op jit(solution)/shard_map/ppermute | solution.py:173
  95.4 60.1 %collective-permute-start.3 = (f32[1280,256]{1,0:T(8,128)}, f32[1280,256]{1,0:T(8,128)}, u32[]{:S(2)}, u32[]{:S(2)}) collective-permute-start(f32[1280,256]{1,0:T(8,128)} %pad_maximum_fusion.2), channel_id=1, source_target_pairs={{0,2},{4,6},{8,10},{12,14},{16,18},{20,22},{24,26},{28,30}} | collective-permute-start | bytes 3932168 | tf_op jit(solution)/shard_map/ppermute | solution.py:173
  122.3 30.9 %collective-permute-start.10 = (f32[256,256]{1,0:T(8,128)}, f32[256,256]{1,0:T(8,128)}, u32[]{:S(2)}, u32[]{:S(2)}) collective-permute-start(f32[256,256]{1,0:T(8,128)} %slice.510), channel_id=1, source_target_pairs={{0,4},{16,20}} | collective-permute-start | bytes 786440 | tf_op jit(solution)/shard_map/ppermute | solution.py:173
  126.0 39.4 %collective-permute-start.6 = (f32[256,1024]{1,0:T(8,128)}, f32[256,1024]{1,0:T(8,128)}, u32[]{:S(2)}, u32[]{:S(2)}) collective-permute-start(f32[256,1024]{1,0:T(8,128)} %broadcast_select_fusion.5), channel_id=1, source_target_pairs={{4,8},{5,9},{6,10},{7,11},{20,24},{21,25},{22,26},{23,27}} | collective-permute-start | bytes 3145736 | tf_op jit(solution)/shard_map/ppermute | solution.py:173
  150.1 1.1 copy-start.10
  151.2 24.6 %collective-permute-start.16 = (f32[256,1024]{1,0:T(8,128)S(1)}, f32[256,1024]{1,0:T(8,128)S(1)}, u32[]{:S(2)}, u32[]{:S(2)}) collective-permute-start(f32[256,1024]{1,0:T(8,128)S(1)} %slice.514), channel_id=1, source_target_pairs={{0,4},{1,5},{2,6},{3,7},{16,20},{17,21},{18,22},{19,23}} | collective-permute-start | bytes 3145736 | tf_op jit(solution)/shard_map/ppermute | solution.py:173
  154.2 9.9 %collective-permute-start.11 = (f32[256,256]{1,0:T(8,128)S(1)}, f32[256,256]{1,0:T(8,128)S(1)}, u32[]{:S(2)}, u32[]{:S(2)}) collective-permute-start(f32[256,256]{1,0:T(8,128)S(1)} %broadcast_select_fusion.12), channel_id=1, source_target_pairs={{4,8},{20,24}} | collective-permute-start | bytes 786440 | tf_op jit(solution)/shard_map/ppermute | solution.py:173
  155.7 23.0 %collective-permute-start.4 = (f32[1280,256]{1,0:T(8,128)S(1)}, f32[1280,256]{1,0:T(8,128)S(1)}, u32[]{:S(2)}, u32[]{:S(2)}) collective-permute-start(f32[1280,256]{1,0:T(8,128)S(1)} %broadcast_select_fusion.1), channel_id=1, source_target_pairs={{0,1},{2,3},{4,5},{6,7},{8,9},{10,11},{12,13},{14,15},{16,17},{18,... | collective-permute-start | bytes 3932168 | tf_op jit(solution)/shard_map/ppermute | solution.py:173
  164.1 8.0 %collective-permute-start.12 = (f32[256,256]{1,0:T(8,128)S(1)}, f32[256,256]{1,0:T(8,128)S(1)}, u32[]{:S(2)}, u32[]{:S(2)}) collective-permute-start(f32[256,256]{1,0:T(8,128)S(1)} %broadcast_select_fusion.14), channel_id=1, source_target_pairs={{8,12},{24,28}} | collective-permute-start | bytes 786440 | tf_op jit(solution)/shard_map/ppermute | solution.py:173
  166.8 6.5 %copy-start.13 = (f32[256,1024]{1,0:T(8,128)}, f32[256,1024]{1,0:T(8,128)S(1)}, u32[]{:S(2)}) copy-start(f32[256,1024]{1,0:T(8,128)S(1)} %broadcast_select_fusion.7) | copy-start | bytes 3145732
  166.9 8.9 %copy-start.11 = (f32[384,1024]{1,0:T(8,128)S(1)}, f32[384,1024]{1,0:T(8,128)}, u32[]{:S(2)}) copy-start(f32[384,1024]{1,0:T(8,128)} %copy-done.10) | copy-start | bytes 4718596
  166.9 40.2 %collective-permute-start.7 = (f32[256,1024]{1,0:T(8,128)S(1)}, f32[256,1024]{1,0:T(8,128)}, u32[]{:S(2)}, u32[]{:S(2)}) collective-permute-start(f32[256,1024]{1,0:T(8,128)S(1)} %broadcast_select_fusion.7), channel_id=1, source_target_pairs={{8,12},{9,13},{10,14},{11,15},{24,28},{25,29},{26,30},{27,31}} | collective-permute-start | bytes 3145736 | tf_op jit(solution)/shard_map/ppermute | solution.py:173
  173.4 40.3 %collective-permute-start.13 = (f32[1280,256]{1,0:T(8,128)}, f32[1280,256]{1,0:T(8,128)}, u32[]{:S(2)}, u32[]{:S(2)}) collective-permute-start(f32[1280,256]{1,0:T(8,128)} %pad_maximum_fusion.3), channel_id=1, source_target_pairs={{0,2},{4,6},{8,10},{12,14},{16,18},{20,22},{24,26},{28,30}} | collective-permute-start | bytes 3932168 | tf_op jit(solution)/shard_map/ppermute | solution.py:173
  176.9 38.7 %collective-permute-start.17 = (f32[256,1024]{1,0:T(8,128)}, f32[256,1024]{1,0:T(8,128)}, u32[]{:S(2)}, u32[]{:S(2)}) collective-permute-start(f32[256,1024]{1,0:T(8,128)} %broadcast_select_fusion.4), channel_id=1, source_target_pairs={{4,8},{5,9},{6,10},{7,11},{20,24},{21,25},{22,26},{23,27}} | collective-permute-start | bytes 3145736 | tf_op jit(solution)/shard_map/ppermute | solution.py:173
  178.9 1.1 copy-start.9
  204.7 2.4 copy-start.15
  207.0 74.7 %copy-start.2 = (f32[1024,256]{1,0:T(8,128)}, f32[1024,256]{1,0:T(8,128)S(1)}, u32[]{:S(2)}) copy-start(f32[1024,256]{1,0:T(8,128)S(1)} %fusion.4.refs_6_) | copy-start | bytes 3145732
  214.1 9.7 %collective-permute-start.14 = (f32[1280,256]{1,0:T(8,128)S(1)}, f32[1280,256]{1,0:T(8,128)S(1)}, u32[]{:S(2)}, u32[]{:S(2)}) collective-permute-start(f32[1280,256]{1,0:T(8,128)S(1)} %broadcast_select_fusion), channel_id=1, source_target_pairs={{0,1},{2,3},{4,5},{6,7},{8,9},{10,11},{12,13},{14,15},{16,17},{18,... | collective-permute-start | bytes 3932168 | tf_op jit(solution)/shard_map/ppermute | solution.py:173
  215.5 2.6 copy-start.17
  218.1 34.6 %collective-permute-start.18 = (f32[256,1024]{1,0:T(8,128)}, f32[256,1024]{1,0:T(8,128)}, u32[]{:S(2)}, u32[]{:S(2)}) collective-permute-start(f32[256,1024]{1,0:T(8,128)} %broadcast_select_fusion.6), channel_id=1, source_target_pairs={{8,12},{9,13},{10,14},{11,15},{24,28},{25,29},{26,30},{27,31}} | collective-permute-start | bytes 3145736 | tf_op jit(solution)/shard_map/ppermute | solution.py:173
  223.8 0.8 copy-start.19
  224.6 1.1 copy-start.8
  250.4 2.4 copy-start.16
  255.0 4.8 %copy-start.4 = (f32[256,1024]{1,0:T(8,128)}, f32[256,1024]{1,0:T(8,128)S(1)}, u32[]{:S(2)}) copy-start(f32[256,1024]{1,0:T(8,128)S(1)} %fusion.6.refs_9_) | copy-start | bytes 3145732
  255.0 2.6 copy-start.20
  258.8 10.8 %copy-start.18 = (f32[128,1024]{1,0:T(8,128)S(1)}, f32[128,1024]{1,0:T(8,128)}, u32[]{:S(2)}) copy-start(f32[128,1024]{1,0:T(8,128)} %copy-done.17) | copy-start | bytes 1572868
  258.8 3.0 collective-permute-start.19
  261.8 11.1 %copy-start = (f32[1,1024,1024]{2,1,0:T(8,128)S(1)}, f32[1,1024,1024]{2,1,0:T(8,128)}, u32[]{:S(2)}) copy-start(f32[1,1024,1024]{2,1,0:T(8,128)} %param.5) | copy-start | bytes 12582916
  261.9 6.4 %collective-permute-start.20 = (f32[128,128]{1,0:T(8,128)S(1)}, f32[128,128]{1,0:T(8,128)S(1)}, u32[]{:S(2)}, u32[]{:S(2)}) collective-permute-start(f32[128,128]{1,0:T(8,128)S(1)} %broadcast_select_fusion.18), channel_id=1, source_target_pairs={{4,8},{20,24}} | collective-permute-start | bytes 196616 | tf_op jit(solution)/shard_map/ppermute | solution.py:173
  268.3 3.2 collective-permute-start.21
  270.8 6.3 %collective-permute-start.24 = (f32[128,1024]{1,0:T(8,128)S(1)}, f32[128,1024]{1,0:T(8,128)S(1)}, u32[]{:S(2)}, u32[]{:S(2)}) collective-permute-start(f32[128,1024]{1,0:T(8,128)S(1)} %select_add_fusion), channel_id=1, source_target_pairs={{0,4},{1,5},{2,6},{3,7},{16,20},{17,21},{18,22},{19,23}} | collective-permute-start | bytes 1572872 | tf_op jit(solution)/shard_map/ppermute | solution.py:173
  271.6 8.7 %collective-permute-start.22 = (f32[1152,128]{1,0:T(8,128)S(1)}, f32[1152,128]{1,0:T(8,128)S(1)}, u32[]{:S(2)}, u32[]{:S(2)}) collective-permute-start(f32[1152,128]{1,0:T(8,128)S(1)} %pad_maximum_fusion.4), channel_id=1, source_target_pairs={{0,2},{4,6},{8,10},{12,14},{16,18},{20,22},{24,26},{28,30}} | collective-permute-start | bytes 1769480 | tf_op jit(solution)/shard_map/ppermute | solution.py:173
  277.1 4.5 %copy-start.21 = (f32[256,256]{1,0:T(8,128)S(1)}, f32[256,256]{1,0:T(8,128)}, u32[]{:S(2)}) copy-start(f32[256,256]{1,0:T(8,128)} %get-tuple-element.20) | copy-start | bytes 786436
  277.2 12.2 %collective-permute-start.25 = (f32[128,1024]{1,0:T(8,128)S(1)}, f32[128,1024]{1,0:T(8,128)S(1)}, u32[]{:S(2)}, u32[]{:S(2)}) collective-permute-start(f32[128,1024]{1,0:T(8,128)S(1)} %broadcast_select_fusion.10), channel_id=1, source_target_pairs={{4,8},{5,9},{6,10},{7,11},{20,24},{21,25},{22,26},{23,27}} | collective-permute-start | bytes 1572872 | tf_op jit(solution)/shard_map/ppermute | solution.py:173
  280.3 12.3 %collective-permute-start.23 = (f32[1152,128]{1,0:T(8,128)S(1)}, f32[1152,128]{1,0:T(8,128)S(1)}, u32[]{:S(2)}, u32[]{:S(2)}) collective-permute-start(f32[1152,128]{1,0:T(8,128)S(1)} %broadcast_select_fusion.8), channel_id=1, source_target_pairs={{0,1},{2,3},{4,5},{6,7},{8,9},{10,11},{12,13},{14,15},{16,17},{18,... | collective-permute-start | bytes 1769480 | tf_op jit(solution)/shard_map/ppermute | solution.py:173
  281.7 1.1 slice-start
  283.7 8.9 %copy-start.12 = (f32[1,1024,1024]{2,1,0:T(8,128)}, f32[1,1024,1024]{2,1,0:T(8,128)S(1)}, u32[]{:S(2)}) copy-start(f32[1,1024,1024]{2,1,0:T(8,128)S(1)} %fusion.1) | copy-start | bytes 12582916
  290.3 17.9 %collective-permute-start.26 = (f32[128,1024]{1,0:T(8,128)}, f32[128,1024]{1,0:T(8,128)}, u32[]{:S(2)}, u32[]{:S(2)}) collective-permute-start(f32[128,1024]{1,0:T(8,128)} %broadcast_select_fusion.11), channel_id=1, source_target_pairs={{8,12},{9,13},{10,14},{11,15},{24,28},{25,29},{26,30},{27,31}} | collective-permute-start | bytes 1572872 | tf_op jit(solution)/shard_map/ppermute | solution.py:173
  292.7 0.8 copy-start.14
  293.5 16.3 %copy-start.3 = (f32[1024,256]{1,0:T(8,128)S(1)}, f32[1024,256]{1,0:T(8,128)}, u32[]{:S(2)}) copy-start(f32[1024,256]{1,0:T(8,128)} %copy-done.2) | copy-start | bytes 3145732
  306.4 3.4 %copy-start.5 = (f32[256,1024]{1,0:T(8,128)S(1)}, f32[256,1024]{1,0:T(8,128)}, u32[]{:S(2)}) copy-start(f32[256,1024]{1,0:T(8,128)} %copy-done.4) | copy-start | bytes 3145732
  306.4 3.4 %copy-start.7 = (f32[128,128]{1,0:T(8,128)S(1)}, f32[128,128]{1,0:T(8,128)}, u32[]{:S(2)}) copy-start(f32[128,128]{1,0:T(8,128)} %get-tuple-element.23.refs_3_) | copy-start | bytes 196612
  309.9 2.2 copy-start.1
  312.1 2.2 copy-start.6

commit v2 on v0

v2 whole, which is shorter than its diff:
```python
import functools

import jax
import jax.numpy as jnp
from jax import lax
from jax.experimental import pallas as pl
from jax.experimental.pallas import tpu as pltpu
from jax.sharding import PartitionSpec as P

BLOCK = 128
CHILD_PANELS = 2
WIDE = BLOCK * CHILD_PANELS
CHUNKS = 4
MESH = pl.DeviceIdType.MESH


def dot(a, b, contract=((1,), (0,))):
    return lax.dot_general(
        a, b, (contract, ((), ())),
        precision=lax.Precision.HIGHEST, preferred_element_type=jnp.float32,
    )


def dot_t(a, b):
    return dot(a, b, ((1,), (1,)))


def factor_block(block, between):
    shape = (BLOCK, BLOCK)
    row = lax.broadcasted_iota(jnp.int32, shape, 0)
    lane = lax.broadcasted_iota(jnp.int32, shape, 1)

    def turn(g, carry):
        m, v = carry
        active = row < BLOCK - 8 * g
        for t in range(8):
            scale = 1.0 / m[t : t + 1, t : t + 1]
            column = jnp.where(active & (row > t), jnp.broadcast_to(m[:, t : t + 1], shape), 0.0)
            pivot_m = m[t : t + 1, :] * scale
            pivot_v = v[t : t + 1, :] * scale
            m = m - column * pivot_m
            v = v - column * pivot_v
        m = pltpu.roll(m, BLOCK - 8, 1)
        m = jnp.concatenate([m[8:], m[:8]], axis=0)
        v = jnp.concatenate([v[8:], v[:8]], axis=0)
        return m, v

    carry = (block, jnp.where(row == lane, 1.0, 0.0))
    half = BLOCK // 16
    carry = lax.fori_loop(0, half, turn, carry)
    between()
    m, v = lax.fori_loop(half, 2 * half, turn, carry)
    between()
    root = 1.0 / jnp.sqrt(jnp.sum(jnp.where(row == lane, m, 0.0), axis=1, keepdims=True))
    return jnp.where(lane >= row, m * root, 0.0), v * root


def kernel(sizes, table, table_send, own, front, child, other, update, tables,
           stage, dbuf, piv, rows, cols, left, right, corr, kbuf, wbuf,
           prow, pcol, ppiv, down_part, across, kp, lprow, lpcol, send_sem, recv_sem):
    leaves, frows, fcols = sizes
    height, breadth = own.shape
    rb, cb = height // BLOCK, breadth // BLOCK
    has_c = rb > CHILD_PANELS and cb > CHILD_PANELS
    l, i, j = lax.axis_index("leaf"), lax.axis_index("frow"), lax.axis_index("fcol")
    top, first = i == 0, j == 0
    corner = top & first
    pending = []
    names = {}

    def sem(*name):
        return recv_sem.at[names.setdefault(name, len(names))]

    def start(cond, src, dst, signal, where):
        copy = pltpu.make_async_remote_copy(
            src_ref=src, dst_ref=dst, send_sem=send_sem.at[len(pending)], recv_sem=signal,
            device_id=where, device_id_type=MESH,
        )
        pending.append((cond, copy))
        pl.when(cond)(copy.start)

    def arrived(cond, dst, signal, where):
        copy = pltpu.make_async_remote_copy(
            src_ref=dst, dst_ref=dst, send_sem=send_sem.at[0], recv_sem=signal,
            device_id=where, device_id_type=MESH,
        )
        pl.when(cond)(copy.wait_recv)

    always = i >= 0
    up = {"frow": lax.rem(i + 1, frows)}
    down = {"frow": lax.rem(i + frows - 1, frows)}
    root_row = {"fcol": lax.rem(j + 1, fcols)}

    def leaf_at(s):
        return {"leaf": lax.rem(l + s, leaves)}

    def rows_of(k):
        return pl.ds(pl.multiple_of(k * BLOCK, BLOCK), BLOCK)

    def chunk(ref, q, count):
        size = ref.shape[0] // count
        return ref.at[pl.ds(q * size, size)]

    barrier = pltpu.get_barrier_semaphore()
    for d in range(1, leaves):
        pl.semaphore_signal(barrier, inc=1, device_id=leaf_at(d), device_id_type=MESH)
    for d in range(1, frows):
        pl.semaphore_signal(barrier, inc=1, device_id={"frow": lax.rem(i + d, frows)}, device_id_type=MESH)
    for d in range(1, fcols):
        pl.semaphore_signal(barrier, inc=1, device_id={"fcol": lax.rem(j + d, fcols)}, device_id_type=MESH)
    pl.semaphore_wait(barrier, leaves + frows + fcols - 3)

    pivot_own = own.at[pl.ds(0, WIDE), pl.ds(0, WIDE)]

    def pivot_of(s):
        return pivot_own if s == 0 else other.at[s - 1, pl.ds(0, WIDE), pl.ds(0, WIDE)]

    def send_pivot(s):
        for b in range(1, frows):
            start(corner, pivot_of(s), dbuf.at[s], sem("d", s), {"frow": b})
        for c in range(1, fcols):
            if c % leaves == s:
                start(corner, pivot_of(s), piv, sem("piv"), {"fcol": c})

    def pass_pivot(s):
        inner = first & (i > 0)
        arrived(inner, dbuf.at[s], sem("d", s), down)
        for c in range(1, fcols):
            if c % leaves == s:
                start(inner, dbuf.at[s], piv, sem("piv"), {"fcol": c})

    send_pivot(0)
    for q in range(CHUNKS):
        start(top, chunk(own.at[pl.ds(0, WIDE)], q, CHUNKS), chunk(cols.at[0], q, CHUNKS), sem("c", 0, q), up)
    for c in range(1, fcols):
        start(first, own.at[:, pl.ds(0, WIDE)], rows.at[0], sem("r", 0), {"fcol": c})

    def is_at(ref, kind, k, t, shape):
        return jnp.broadcast_to(ref[kind, pl.ds(k, 1), 0:1], shape) == t

    def chosen(ref, kind, k, count, block):
        total = 0.0
        for t in range(count):
            part = block(t)
            total = total + jnp.where(is_at(ref, kind, k, t, part.shape), part, 0.0)
        return total

    def stage_rows(r, carry):
        stage[rows_of(r), :] = own[rows_of(r), :]
        return carry

    def block_slice(t):
        return slice(t * BLOCK, (t + 1) * BLOCK)

    def stage_cols(r, carry):
        held = stage[rows_of(r), block_slice(CHILD_PANELS)]
        value = held
        for t in range(CHILD_PANELS + 1, cb):
            here = stage[rows_of(r), block_slice(t)]
            match = is_at(table, 1, 0, t, here.shape)
            value = jnp.where(match, here, value)
            stage[rows_of(r), block_slice(t)] = jnp.where(match, held, here)
        stage[rows_of(r), block_slice(CHILD_PANELS)] = value
        return carry

    pieces = [(0, WIDE, 0, WIDE), (0, WIDE, WIDE, breadth)]
    early, late = 2, []
    if height > WIDE:
        three = WIDE + BLOCK
        pieces += [(WIDE, three, 0, breadth)]
        if height > three:
            pieces += [(three, height, 0, three), (three, height, three, breadth)]

    def piece(ref, n):
        a, b, c, d = pieces[n]
        return ref.at[pl.ds(a, b - a), pl.ds(c, d - c)]

    def send_pieces(numbers):
        for n in numbers:
            for s in range(1, leaves):
                start(always, piece(stage, n), piece(other.at[s - 1], n), sem("y", s, n), leaf_at(s))

    def wait_pieces(numbers):
        for n in numbers:
            for s in range(1, leaves):
                arrived(always, piece(other.at[s - 1], n), sem("y", s, n), leaf_at(leaves - s))

    for s in range(1, leaves):
        start(always, table_send, tables.at[s - 1], sem("tables", s), leaf_at(s))
    lax.fori_loop(0, CHILD_PANELS, stage_rows, 0)
    if has_c:
        @pl.when(first)
        def _():
            lax.fori_loop(0, CHILD_PANELS, stage_cols, 0)
    send_pieces(range(2))
    lax.fori_loop(CHILD_PANELS, rb, stage_rows, 0)
    if has_c:
        @pl.when(top)
        def _():
            def fix(c, carry):
                held = own[block_slice(CHILD_PANELS), rows_of(c)]
                value = held
                for t in range(CHILD_PANELS + 1, rb):
                    here = own[block_slice(t), rows_of(c)]
                    match = is_at(table, 0, 0, t, here.shape)
                    value = jnp.where(match, here, value)
                    stage[block_slice(t), rows_of(c)] = jnp.where(match, held, here)
                stage[block_slice(CHILD_PANELS), rows_of(c)] = value
                return carry

            lax.fori_loop(0, cb, fix, 0)

        @pl.when(first)
        def _():
            lax.fori_loop(CHILD_PANELS, rb, stage_cols, 0)
    send_pieces(range(2, len(pieces)))
    middle = list(range(2, min(4, len(pieces))))
    last = list(range(4, len(pieces)))

    @pl.when(top)
    def _():
        cols[0] = own[0:WIDE, :]

    @pl.when(first)
    def _():
        rows[0] = own[:, 0:WIDE]

    pass_pivot(0)

    @pl.when(corner)
    def _():
        piv[...] = own[0:WIDE, 0:WIDE]

    @pl.when(first & (i > 0))
    def _():
        piv[...] = dbuf[0]

    def pass_cols(s, q):
        here = chunk(cols.at[s], q, CHUNKS)
        arrived(i > 0, here, sem("c", s, q), down)
        start((i > 0) & (i < frows - 1), here, here, sem("c", s, q), up)

    for q in range(CHUNKS):
        pass_cols(0, q)

    wait_pieces(range(2))
    for s in range(1, leaves):
        send_pivot(s)
    for s in range(1, leaves):
        for q in range(CHUNKS):
            source = chunk(other.at[s - 1, pl.ds(0, WIDE)], q, CHUNKS)
            start(top, source, chunk(cols.at[s], q, CHUNKS), sem("c", s, q), up)
        pass_pivot(s)

        @pl.when(top)
        def _(s=s):
            cols[s] = other[s - 1, 0:WIDE, :]

    arrived(j > 0, piv, sem("piv"), root_row)
    slot = lax.rem(j, leaves)
    base = j - slot
    step = []

    def between():
        q = len(step)
        step.append(q)
        for s in range(1, leaves):
            pass_cols(s, q)
        if q == 1:
            wait_pieces(middle)
            for s in range(1, leaves):
                @pl.when(first)
                def _(s=s):
                    rows[s] = other[s - 1, :, 0:WIDE]

                for c in range(1, fcols):
                    start(first, other.at[s - 1, :, pl.ds(0, WIDE)], rows.at[s], sem("r", s), {"fcol": c})

    lo, hi = slice(0, BLOCK), slice(BLOCK, WIDE)
    upper, inverse = factor_block(piv[lo, lo], between)
    kbuf[...] = jnp.zeros_like(kbuf)
    kbuf[lo, lo] = upper.T
    wbuf[slot, lo, lo] = inverse
    wbuf[slot, lo, hi] = jnp.zeros((BLOCK, BLOCK), jnp.float32)
    below = dot_t(piv[hi, lo], inverse)
    kbuf[hi, lo] = below
    upper, second = factor_block(piv[hi, hi] - dot_t(below, below), between)
    kbuf[hi, hi] = upper.T
    wbuf[slot, hi, hi] = second
    wbuf[slot, hi, lo] = -dot(second, dot(below, inverse))
    w_sems = [sem("w", s) for s in range(leaves)]
    w_first = names[("w", 0)]
    for d in range(1, leaves):
        start(always, wbuf.at[slot], wbuf.at[slot], recv_sem.at[w_first + slot], {"fcol": base + lax.rem(slot + d, leaves)})
    for d in range(1, leaves):
        from_slot = lax.rem(slot + d, leaves)
        arrived(always, wbuf.at[from_slot], recv_sem.at[w_first + from_slot], {"fcol": base + from_slot})

    for s in range(1, leaves):
        arrived(always, tables.at[s - 1], sem("tables", s), leaf_at(leaves - s))

    def make_panels(s):
        if s:
            arrived(j > 0, rows.at[s], sem("r", s), root_row)

        def one_row(r, carry):
            left[s, rows_of(r), :] = dot_t(rows[s, rows_of(r), :], wbuf[s])
            return carry

        def one_col(c, carry):
            right[s, :, rows_of(c)] = dot(wbuf[s], cols[s, :, rows_of(c)])
            return carry

        lax.fori_loop(0, rb, one_row, 0)
        lax.fori_loop(0, cb, one_col, 0)

    arrived(j > 0, rows.at[0], sem("r", 0), root_row)
    for s in range(leaves):
        make_panels(s)

    third = block_slice(CHILD_PANELS)
    known = [table] + [tables.at[s - 1] for s in range(1, leaves)]

    @pl.when(first)
    def _():
        for s in range(leaves if has_c else 0):
            if s == 0:
                beside = chosen(table, 1, 0, cb, lambda t: right[0, :, block_slice(t)])
            else:
                beside = right[s, :, third]
                beside = jnp.where(is_at(known[s], 1, 0, CHILD_PANELS, beside.shape), beside, 0.0)

            def one(r, carry, s=s, beside=beside):
                if s == 0:
                    raw = chosen(table, 1, 0, cb, lambda t: own[rows_of(r), block_slice(t)])
                else:
                    raw = other[s - 1, rows_of(r), third]
                    raw = jnp.where(is_at(known[s], 1, 0, CHILD_PANELS, raw.shape), raw, 0.0)
                down_part[s, rows_of(r), :] = raw - dot(left[s, rows_of(r), :], beside)
                return carry

            lax.fori_loop(0, rb, one, 0)

        def assemble(r, carry):
            tile = front[rows_of(r), 0:BLOCK]
            for s in range(leaves if has_c else 0):
                tile = tile + chosen(known[s], 0, r, rb, lambda t: down_part[s, block_slice(t), :])
            prow[rows_of(r), :] = tile
            return carry

        lax.fori_loop(0, rb, assemble, 0)

    @pl.when(top)
    def _():
        for s in range(leaves if has_c else 0):
            if s == 0:
                beside = chosen(table, 0, 0, rb, lambda t: left[0, block_slice(t), :])
            else:
                beside = left[s, third, :]
                beside = jnp.where(is_at(known[s], 0, 0, CHILD_PANELS, beside.shape), beside, 0.0)

            def one(c, carry, s=s, beside=beside):
                if s == 0:
                    raw = chosen(table, 0, 0, rb, lambda t: own[block_slice(t), rows_of(c)])
                else:
                    raw = other[s - 1, third, rows_of(c)]
                    raw = jnp.where(is_at(known[s], 0, 0, CHILD_PANELS, raw.shape), raw, 0.0)
                across[s, :, rows_of(c)] = raw - dot(beside, right[s, :, rows_of(c)])
                return carry

            lax.fori_loop(0, cb, one, 0)

        def assemble(c, carry):
            tile = front[0:BLOCK, rows_of(c)]
            for s in range(leaves if has_c else 0):
                tile = tile + chosen(known[s], 1, c, cb, lambda t: across[s, :, block_slice(t)])
            pcol[:, rows_of(c)] = tile
            return carry

        lax.fori_loop(0, cb, assemble, 0)

    @pl.when(corner)
    def _():
        ppiv[...] = prow[0:BLOCK, :]

    for b in range(1, frows):
        start(corner, ppiv, ppiv, sem("pp"), {"frow": b})
    for c in range(1, fcols):
        start(corner, ppiv, ppiv, sem("pp"), {"fcol": c})
    for q in range(2):
        start(top, chunk(pcol, q, 2), chunk(pcol, q, 2), sem("pc", q), up)
    for c in range(1, fcols):
        start(first, prow, prow, sem("pr"), {"fcol": c})
    arrived(first & (i > 0), ppiv, sem("pp"), down)
    for c in range(1, fcols):
        start(first & (i > 0), ppiv, ppiv, sem("pp"), {"fcol": c})

    def child_row(r, carry):
        value = own[rows_of(r), :] - dot(left[0, rows_of(r), :], right[0])
        child[rows_of(r), :] = jnp.where(top & (r < CHILD_PANELS), 0.0, value)
        return carry

    lax.fori_loop(0, rb, child_row, 0)

    @pl.when(first)
    def _():
        child[:, 0:WIDE] = left[0]

    @pl.when(corner)
    def _():
        child[0:WIDE, 0:WIDE] = kbuf[...]

    arrived(j > 0, ppiv, sem("pp"), root_row)
    turn = []

    def pass_parent():
        q = len(turn)
        turn.append(q)
        part = chunk(pcol, q, 2)
        arrived(i > 0, part, sem("pc", q), down)
        start((i > 0) & (i < frows - 1), part, part, sem("pc", q), up)

    upper, inverse = factor_block(ppiv[...], pass_parent)
    kp[...] = upper.T
    for s in range(1, leaves):
        def corr_row(r, carry, s=s):
            corr[s - 1, rows_of(r), :] = dot(left[s, rows_of(r), :], right[s])
            return carry

        lax.fori_loop(0, rb, corr_row, 0)
    arrived(j > 0, prow, sem("pr"), root_row)
    lprow[...] = dot_t(prow[...], inverse)
    lpcol[...] = dot(inverse, pcol[...])

    def parent_row(r, carry):
        value = front[rows_of(r), :] - dot(lprow[rows_of(r), :], lpcol[...])
        update[rows_of(r), :] = jnp.where(top & (r == 0), 0.0, value)
        return carry

    lax.fori_loop(0, rb, parent_row, 0)

    @pl.when(first)
    def _():
        update[:, 0:BLOCK] = lprow[...]

    @pl.when(corner)
    def _():
        update[0:BLOCK, 0:BLOCK] = kp[...]

    wait_pieces(last)

    for cond, copy in pending:
        pl.when(cond)(copy.wait_send)

    def subtract(r, carry):
        for s in range(1, leaves):
            other[s - 1, rows_of(r), :] = other[s - 1, rows_of(r), :] - corr[s - 1, rows_of(r), :]
        return carry

    lax.fori_loop(0, rb, subtract, 0)


def assemble_kernel(children, sources, where_am_i, update, *refs):
    blocks, out = refs[:children], refs[children]
    r = pl.program_id(0)
    for c in range(out.shape[1] // BLOCK):
        span = slice(c * BLOCK, (c + 1) * BLOCK)
        tile = update[:, span]
        panel = (where_am_i[0] + r == 0) | ((where_am_i[1] == 0) & (c == 0))
        for s in range(children):
            source = sources[s, 1, c]
            keep = (sources[s, 0, r] >= 0) & (source >= 0) & jnp.logical_not(panel)
            at = pl.ds(pl.multiple_of(jnp.maximum(source, 0) * BLOCK, BLOCK), BLOCK)
            tile = tile + jnp.where(keep, blocks[s][:, at], 0.0)
        out[:, span] = tile


def assemble(sources, where_am_i, update, blocks):
    height, breadth = update.shape
    children = len(blocks)

    def moved(s):
        return lambda r, sources, where_am_i: (jnp.maximum(sources[s, 0, r], 0), 0)

    row = pl.BlockSpec((BLOCK, breadth), lambda r, sources, where_am_i: (r, 0))
    return pl.pallas_call(
        functools.partial(assemble_kernel, children),
        grid_spec=pltpu.PrefetchScalarGridSpec(
            num_scalar_prefetch=2,
            grid=(height // BLOCK,),
            in_specs=[row] + [pl.BlockSpec((BLOCK, breadth), moved(s)) for s in range(children)],
            out_specs=row,
        ),
        out_shape=jax.ShapeDtypeStruct((height, breadth), jnp.float32),
        name="assemble",
    )(sources, where_am_i, update, *blocks)


def per_device(sizes, child_fronts, parent_front, block_maps):
    leaves, frows, fcols = sizes
    height, breadth = parent_front.shape
    assert fcols % leaves == 0
    rb, cb = height // BLOCK, breadth // BLOCK
    i, j = lax.axis_index("frow"), lax.axis_index("fcol")
    number = jnp.arange(block_maps.shape[1], dtype=jnp.int32)
    matches = block_maps[0][:, None] == number[None, :]
    inverse = jnp.sum(jnp.where(matches, number[:, None], 0), axis=0)
    deep = -(-max(rb, cb) // 8) * 8
    own_lines, sent_lines = [], []
    for count, position in ((rb, i), (cb, j)):
        source = lax.dynamic_slice_in_dim(inverse, position * count, count)
        kept = source >= CHILD_PANELS
        source = source - position * count
        to = jnp.maximum(inverse[0], CHILD_PANELS)
        swapped = jnp.where(source == to, CHILD_PANELS, jnp.where(source == CHILD_PANELS, to, source))
        swap = (position == 0) & (min(rb, cb) > CHILD_PANELS)
        swapped = jnp.where(swap, swapped, source)
        for lines, values in ((own_lines, source), (sent_lines, swapped)):
            lines.append(jnp.pad(jnp.where(kept, values, -1), (0, deep - count)))
    table, table_send = (
        jnp.broadcast_to(jnp.stack(lines)[:, :, None], (2, deep, BLOCK)) for lines in (own_lines, sent_lines)
    )
    f32 = jnp.float32
    block = jax.ShapeDtypeStruct((height, breadth), f32)
    vmem = pl.BlockSpec(memory_space=pltpu.VMEM)
    sends = (
        leaves * (frows - 1) + 2 * fcols + leaves * CHUNKS * 2 + leaves * fcols + leaves * 7
        + frows + fcols * 3 + 4 + fcols * leaves
    )
    square = (BLOCK, BLOCK)
    scratch = [
        pltpu.VMEM((height, breadth), f32),
        pltpu.VMEM((leaves, WIDE, WIDE), f32),
        pltpu.VMEM((WIDE, WIDE), f32),
        pltpu.VMEM((leaves, height, WIDE), f32),
        pltpu.VMEM((leaves, WIDE, breadth), f32),
        pltpu.VMEM((leaves, height, WIDE), f32),
        pltpu.VMEM((leaves, WIDE, breadth), f32),
        pltpu.VMEM((leaves - 1, height, breadth), f32),
        pltpu.VMEM((WIDE, WIDE), f32),
        pltpu.VMEM((leaves, WIDE, WIDE), f32),
        pltpu.VMEM((height, BLOCK), f32),
        pltpu.VMEM((BLOCK, breadth), f32),
        pltpu.VMEM(square, f32),
        pltpu.VMEM((leaves, height, BLOCK), f32),
        pltpu.VMEM((leaves, BLOCK, breadth), f32),
        pltpu.VMEM(square, f32),
        pltpu.VMEM((height, BLOCK), f32),
        pltpu.VMEM((BLOCK, breadth), f32),
        pltpu.SemaphoreType.DMA((sends,)),
        pltpu.SemaphoreType.DMA((leaves * 14 + 10,)),
    ]
    child, other, update, tables = pl.pallas_call(
        functools.partial(kernel, sizes),
        out_shape=(
            block,
            jax.ShapeDtypeStruct((leaves - 1, height, breadth), f32),
            block,
            jax.ShapeDtypeStruct((leaves - 1, 2, deep, BLOCK), jnp.int32),
        ),
        in_specs=[vmem] * 4,
        out_specs=(vmem,) * 4,
        scratch_shapes=scratch,
        compiler_params=pltpu.CompilerParams(
            collective_id=0, has_side_effects=True, vmem_limit_bytes=56 * 2**20
        ),
        name="fronts",
    )(table, table_send, child_fronts[0], parent_front)
    sources = jnp.concatenate([table[None], tables], axis=0)[:, :, :, 0]
    where_am_i = jnp.stack([i, j]).astype(jnp.int32)
    parent = assemble(sources, where_am_i, update, [child] + [other[s] for s in range(leaves - 1)])
    return child[None], parent


def solution(mesh):
    sizes = (mesh.shape["leaf"], mesh.shape["frow"], mesh.shape["fcol"])
    return jax.shard_map(
        functools.partial(per_device, sizes),
        mesh=mesh,
        in_specs=(P("leaf", "frow", "fcol"), P("frow", "fcol"), P("leaf", None)),
        out_specs=(P("leaf", "frow", "fcol"), P("frow", "fcol")),
        check_vma=False,
    )
```

time: 627 us -> 175 us (0.28); the launches traced: 616 us -> 174 us
  waiting for transfers between devices: 414 us -> 0 us
  Pallas kernels: 0 us -> 164 us
  other arithmetic: 95.4 us -> 2.92 us
  local copies, waits for them, and re-layouts: 61.6 us -> 6.19 us
  matrix products: 29 us -> 0 us
  between operations: 15.1 us -> 0.7 us
    psum x10 -> x0, waiting for transfers between devices: 414 us -> none  [the longest x6 200 us: from_root(): return lax.psum(jnp.where(mine, shard, jnp.zeros_like(shard)), axis)]
    pallas_call x0 -> x2, Pallas kernels: none -> 164 us  [the longest x1 155 us: per_device(): pl.pallas_call(functools.partial(kernel, sizes), out_shape=(block, jax.Sh...]
    another operation x17 -> x3, other arithmetic: 69.9 us -> 0.75 us  [the longest x1 0.65 us: per_device(): where_am_i = jnp.stack([i, j]).astype(jnp.int32)]
    gather x9 -> x0, local copies, waits for them, and re-layouts: 24.3 us -> none  [the longest x2 10.3 us: extend_frame(): tile_grid = jnp.take(tile_grid, col_source, axis=2)]
    unnamed x19 -> x1, local copies, waits for them, and re-layouts: 28.8 us -> 4.79 us
    dot_general x3 -> x0, matrix products: 21.4 us -> none  [factor_panels(): update = jnp.dot(shared, across.T, precision=lax.Precision.HIGHEST)]
    select_n x11 -> x0, other arithmetic: 11 us -> none  [the longest x3 5.67 us: factor_panels(): jnp.where(inside, shared, 0.0)]
    another operation x3 -> x0, matrix products: 7.62 us -> none  [factor_panels(): lax.linalg.triangular_solve(factor, column, left_side=False, lower=True,...]
  transfers between devices with their start and end apart: 10 -> 0, of which waited for: 10 -> 0; matrix products, arithmetic and copies ran while one was open for 2% -> 0% of each run, Pallas kernels for 0% -> 0%
where the time goes in v2:
time: 175 us; the launch traced here: 174 us
  Pallas kernels  164 us (94%)
  local copies, waits for them, and re-layouts  6.19 us (4%)
  other arithmetic  2.92 us (2%)
    pallas_call x1, Pallas kernels, per_device(): pl.pallas_call(functools.partial(kernel, sizes), out_shape=(block, jax.Sh...  155 us
    pallas_call x1, Pallas kernels, assemble(): pl.pallas_call(functools.partial(assemble_kernel, children), grid_spec=pl...  9.53 us
    unnamed x1, local copies, waits for them, and re-layouts  4.79 us

profile of v2, /device:TPU:31, one launch (start us, length us, event | category | flops | bytes accessed | tf_op | source)
XLA Modules:
  0.0 173.9 jit_solution(4505095360177671042)
XLA Ops:
  0.6 0.7 select_reduce_fusion
  1.4 0.1 fusion.3
  1.5 0.7 pad_add_fusion.3.where_am_i
  2.2 0.7 broadcast_in_dim.46.table_send
  2.9 0.1 broadcast_in_dim_broadcast_in_dim.2
  2.9 0.7 broadcast_in_dim.45.table
  3.6 154.6 %fronts.1 = (f32[1024,1024]{1,0:T(8,128)}, f32[1,1024,1024]{2,1,0:T(8,128)}, f32[1024,1024]{1,0:T(8,128)}, s32[1,2,8,128]{3,2,1,0:T(8,128)}) custom-call(s32[2,8,128]{2,1,0:T(8,128)} %broadcast_in_dim.45.table, s32[2,8,128]{2,1,0:T(8,128)} %broadcast_in_dim.46.table_send, f32[1024,1024]{1,0:T(8,128)} %bitcast.17, f32[1024,1024]{1,0:T(8,128)} %front.1), custom_call_target="tpu_custom_call" | custom-call | tf_op jit(solution)/shard_map/fronts/pallas_call | solution.py:553
  158.2 1.4 fusion.sources
  159.6 9.5 %assemble.1 = f32[1024,1024]{1,0:T(8,128)} custom-call(s32[2,2,8]{2,1,0:T(2,128)} %fusion.sources, s32[2]{0:T(128)} %pad_add_fusion.3.where_am_i, f32[1024,1024]{1,0:T(8,128)} %get-tuple-element.8.update, f32[1024,1024]{1,0:T(8,128)} %get-tuple-element.6.refs_0_, f32[1024,1024]{1,0:T(8,128)} %bitcast.18), custom_call_target="tpu_custom_call" | custom-call | tf_op jit(solution)/shard_map/assemble/pallas_call | solution.py:486
  169.1 4.8 %copy.6 = f32[1,1024,1024]{2,1,0:T(8,128)} copy(f32[1,1024,1024]{2,1,0:T(8,128)} %bitcast.16) | data formatting | bytes 8388608
  (1 shorter events, 0.0 us)

commit v3 on v2

--- a/solution.py
+++ b/solution.py
@@ -23,6 +23,20 @@
 
 def dot_t(a, b):
     return dot(a, b, ((1,), (1,)))
+
+
+def split(x):
+    high = x.astype(jnp.bfloat16)
+    return high, (x - high.astype(jnp.float32)).astype(jnp.bfloat16)
+
+
+def dot_split(a, high, low):
+    a_high, a_low = split(a)
+
+    def one(x, y):
+        return lax.dot_general(x, y, (((1,), (0,)), ((), ())), preferred_element_type=jnp.float32)
+
+    return one(a_high, high) + (one(a_high, low) + one(a_low, high))
 
 
 def factor_block(block, between):
@@ -46,18 +60,18 @@
         return m, v
 
     carry = (block, jnp.where(row == lane, 1.0, 0.0))
-    half = BLOCK // 16
-    carry = lax.fori_loop(0, half, turn, carry)
-    between()
-    m, v = lax.fori_loop(half, 2 * half, turn, carry)
-    between()
+    turns = BLOCK // 8 // CHUNKS
+    for q in range(CHUNKS):
+        carry = lax.fori_loop(q * turns, (q + 1) * turns, turn, carry)
+        between()
+    m, v = carry
     root = 1.0 / jnp.sqrt(jnp.sum(jnp.where(row == lane, m, 0.0), axis=1, keepdims=True))
     return jnp.where(lane >= row, m * root, 0.0), v * root
 
 
-def kernel(sizes, table, table_send, own, front, child, other, update, tables,
+def kernel(sizes, table, table_send, own, front_hbm, child_hbm, other, update_hbm, tables,
            stage, dbuf, piv, rows, cols, left, right, corr, kbuf, wbuf,
-           prow, pcol, ppiv, down_part, across, kp, lprow, lpcol, send_sem, recv_sem):
+           prow, pcol, ppiv, down_part, across, kp, lprow, lpcol, front, child, update, high, low, send_sem, recv_sem, local_sem):
     leaves, frows, fcols = sizes
     height, breadth = own.shape
     rb, cb = height // BLOCK, breadth // BLOCK
@@ -100,6 +114,9 @@
     def chunk(ref, q, count):
         size = ref.shape[0] // count
         return ref.at[pl.ds(q * size, size)]
+
+    load = pltpu.make_async_copy(front_hbm, front, local_sem.at[0])
+    load.start()
 
     barrier = pltpu.get_barrier_semaphore()
     for d in range(1, leaves):
@@ -163,22 +180,23 @@
         stage[rows_of(r), block_slice(CHILD_PANELS)] = value
         return carry
 
+    three = WIDE + BLOCK
     pieces = [(0, WIDE, 0, WIDE), (0, WIDE, WIDE, breadth)]
-    early, late = 2, []
     if height > WIDE:
-        three = WIDE + BLOCK
-        pieces += [(WIDE, three, 0, breadth)]
-        if height > three:
-            pieces += [(three, height, 0, three), (three, height, three, breadth)]
+        pieces += [(WIDE, height, 0, WIDE), (WIDE, three, WIDE, breadth)]
+    if height > three:
+        pieces += [(three, height, WIDE, three), (three, height, three, breadth)]
+    panel, middle, last = [2], [3, 4], [5]
+    panel, middle, last = ([n for n in some if n < len(pieces)] for some in (panel, middle, last))
 
     def piece(ref, n):
         a, b, c, d = pieces[n]
         return ref.at[pl.ds(a, b - a), pl.ds(c, d - c)]
 
-    def send_pieces(numbers):
+    def send_pieces(numbers, cond=always, source=stage):
         for n in numbers:
             for s in range(1, leaves):
-                start(always, piece(stage, n), piece(other.at[s - 1], n), sem("y", s, n), leaf_at(s))
+                start(cond, piece(source, n), piece(other.at[s - 1], n), sem("y", s, n), leaf_at(s))
 
     def wait_pieces(numbers):
         for n in numbers:
@@ -187,12 +205,14 @@
 
     for s in range(1, leaves):
         start(always, table_send, tables.at[s - 1], sem("tables", s), leaf_at(s))
+    send_pieces([0], source=own)
+    send_pieces(panel, i > 0, own)
     lax.fori_loop(0, CHILD_PANELS, stage_rows, 0)
     if has_c:
         @pl.when(first)
         def _():
             lax.fori_loop(0, CHILD_PANELS, stage_cols, 0)
-    send_pieces(range(2))
+    send_pieces([1], top)
     lax.fori_loop(CHILD_PANELS, rb, stage_rows, 0)
     if has_c:
         @pl.when(top)
@@ -213,9 +233,12 @@
         @pl.when(first)
         def _():
             lax.fori_loop(CHILD_PANELS, rb, stage_cols, 0)
-    send_pieces(range(2, len(pieces)))
-    middle = list(range(2, min(4, len(pieces))))
-    last = list(range(4, len(pieces)))
+    send_pieces(panel, top)
+    send_pieces(middle[1:], i > 0)
+    send_pieces([1], i > 0)
+    send_pieces(middle, top)
+    send_pieces(middle[:1], i > 0)
+    send_pieces(last)
 
     @pl.when(top)
     def _():
@@ -234,27 +257,19 @@
     @pl.when(first & (i > 0))
     def _():
         piv[...] = dbuf[0]
+
+    inner_rows = (i > 0) & (i < frows - 1)
 
     def pass_cols(s, q):
         here = chunk(cols.at[s], q, CHUNKS)
-        arrived(i > 0, here, sem("c", s, q), down)
-        start((i > 0) & (i < frows - 1), here, here, sem("c", s, q), up)
-
-    for q in range(CHUNKS):
-        pass_cols(0, q)
-
-    wait_pieces(range(2))
+        arrived(inner_rows, here, sem("c", s, q), down)
+        start(inner_rows, here, here, sem("c", s, q), up)
+
+    wait_pieces([0])
     for s in range(1, leaves):
         send_pivot(s)
     for s in range(1, leaves):
-        for q in range(CHUNKS):
-            source = chunk(other.at[s - 1, pl.ds(0, WIDE)], q, CHUNKS)
-            start(top, source, chunk(cols.at[s], q, CHUNKS), sem("c", s, q), up)
         pass_pivot(s)
-
-        @pl.when(top)
-        def _(s=s):
-            cols[s] = other[s - 1, 0:WIDE, :]
 
     arrived(j > 0, piv, sem("piv"), root_row)
     slot = lax.rem(j, leaves)
@@ -262,19 +277,33 @@
     step = []
 
     def between():
-        q = len(step)
-        step.append(q)
-        for s in range(1, leaves):
-            pass_cols(s, q)
-        if q == 1:
-            wait_pieces(middle)
+        n = len(step)
+        step.append(n)
+        q = n % CHUNKS
+        if n < CHUNKS:
+            pass_cols(0, q)
+        else:
             for s in range(1, leaves):
+                pass_cols(s, q)
+        if n == CHUNKS - 1:
+            wait_pieces([1])
+            for s in range(1, leaves):
+                for p in range(CHUNKS):
+                    source = chunk(other.at[s - 1, pl.ds(0, WIDE)], p, CHUNKS)
+                    start(top, source, chunk(cols.at[s], p, CHUNKS), sem("c", s, p), up)
+
+                @pl.when(top)
+                def _(s=s):
+                    cols[s] = other[s - 1, 0:WIDE, :]
+        if n == CHUNKS + 1:
+            wait_pieces(panel)
+            for s in range(1, leaves):
+                for c in range(1, fcols):
+                    start(first, other.at[s - 1, :, pl.ds(0, WIDE)], rows.at[s], sem("r", s), {"fcol": c})
+
                 @pl.when(first)
                 def _(s=s):
                     rows[s] = other[s - 1, :, 0:WIDE]
-
-                for c in range(1, fcols):
-                    start(first, other.at[s - 1, :, pl.ds(0, WIDE)], rows.at[s], sem("r", s), {"fcol": c})
 
     lo, hi = slice(0, BLOCK), slice(BLOCK, WIDE)
     upper, inverse = factor_block(piv[lo, lo], between)
@@ -300,23 +329,48 @@
         arrived(always, tables.at[s - 1], sem("tables", s), leaf_at(leaves - s))
 
     def make_panels(s):
-        if s:
-            arrived(j > 0, rows.at[s], sem("r", s), root_row)
+        arrived(j > 0, rows.at[s], sem("r", s), root_row)
+        for q in range(CHUNKS):
+            arrived(i == frows - 1, chunk(cols.at[s], q, CHUNKS), sem("c", s, q), down)
+
+        def wide(k):
+            return pl.ds(pl.multiple_of(k * WIDE, WIDE), WIDE)
 
         def one_row(r, carry):
-            left[s, rows_of(r), :] = dot_t(rows[s, rows_of(r), :], wbuf[s])
+            left[s, wide(r), :] = dot_t(rows[s, wide(r), :], wbuf[s])
             return carry
 
         def one_col(c, carry):
-            right[s, :, rows_of(c)] = dot(wbuf[s], cols[s, :, rows_of(c)])
+            right[s, :, wide(c)] = dot(wbuf[s], cols[s, :, wide(c)])
             return carry
 
-        lax.fori_loop(0, rb, one_row, 0)
-        lax.fori_loop(0, cb, one_col, 0)
-
-    arrived(j > 0, rows.at[0], sem("r", 0), root_row)
-    for s in range(leaves):
+        lax.fori_loop(0, height // WIDE, one_row, 0)
+        lax.fori_loop(0, breadth // WIDE, one_col, 0)
+
+    make_panels(0)
+    high[...], low[...] = split(right[0])
+
+    def child_row(r, carry):
+        value = own[rows_of(r), :] - dot_split(left[0, rows_of(r), :], high[...], low[...])
+        child[rows_of(r), :] = jnp.where(top & (r < CHILD_PANELS), 0.0, value)
+        return carry
+
+    lax.fori_loop(0, rb, child_row, 0)
+
+    @pl.when(first)
+    def _():
+        child[:, 0:WIDE] = left[0]
+
+    @pl.when(corner)
+    def _():
+        child[0:WIDE, 0:WIDE] = kbuf[...]
+
+    child_copy = pltpu.make_async_copy(child, child_hbm, local_sem.at[1])
+    child_copy.start()
+    for s in range(1, leaves):
         make_panels(s)
+    wait_pieces(middle)
+    load.wait()
 
     third = block_slice(CHILD_PANELS)
     known = [table] + [tables.at[s - 1] for s in range(1, leaves)]
@@ -395,45 +449,37 @@
     for c in range(1, fcols):
         start(first & (i > 0), ppiv, ppiv, sem("pp"), {"fcol": c})
 
-    def child_row(r, carry):
-        value = own[rows_of(r), :] - dot(left[0, rows_of(r), :], right[0])
-        child[rows_of(r), :] = jnp.where(top & (r < CHILD_PANELS), 0.0, value)
-        return carry
-
-    lax.fori_loop(0, rb, child_row, 0)
-
-    @pl.when(first)
-    def _():
-        child[:, 0:WIDE] = left[0]
-
-    @pl.when(corner)
-    def _():
-        child[0:WIDE, 0:WIDE] = kbuf[...]
+    for s in range(1, leaves):
+        high[...], low[...] = split(right[s])
+
+        def corr_row(r, carry, s=s):
+            corr[s - 1, rows_of(r), :] = dot_split(left[s, rows_of(r), :], high[...], low[...])
+            return carry
+
+        lax.fori_loop(0, rb, corr_row, 0)
 
     arrived(j > 0, ppiv, sem("pp"), root_row)
     turn = []
 
     def pass_parent():
-        q = len(turn)
-        turn.append(q)
-        part = chunk(pcol, q, 2)
-        arrived(i > 0, part, sem("pc", q), down)
-        start((i > 0) & (i < frows - 1), part, part, sem("pc", q), up)
+        n = len(turn)
+        turn.append(n)
+        if n % 2 == 0:
+            part = chunk(pcol, n // 2, 2)
+            arrived(inner_rows, part, sem("pc", n // 2), down)
+            start(inner_rows, part, part, sem("pc", n // 2), up)
 
     upper, inverse = factor_block(ppiv[...], pass_parent)
     kp[...] = upper.T
-    for s in range(1, leaves):
-        def corr_row(r, carry, s=s):
-            corr[s - 1, rows_of(r), :] = dot(left[s, rows_of(r), :], right[s])
-            return carry
-
-        lax.fori_loop(0, rb, corr_row, 0)
+    for q in range(2):
+        arrived(i == frows - 1, chunk(pcol, q, 2), sem("pc", q), down)
     arrived(j > 0, prow, sem("pr"), root_row)
     lprow[...] = dot_t(prow[...], inverse)
     lpcol[...] = dot(inverse, pcol[...])
+    high[0:BLOCK, :], low[0:BLOCK, :] = split(lpcol[...])
 
     def parent_row(r, carry):
-        value = front[rows_of(r), :] - dot(lprow[rows_of(r), :], lpcol[...])
+        value = front[rows_of(r), :] - dot_split(lprow[rows_of(r), :], high[0:BLOCK, :], low[0:BLOCK, :])
         update[rows_of(r), :] = jnp.where(top & (r == 0), 0.0, value)
         return carry
 
@@ -447,6 +493,8 @@
     def _():
         update[0:BLOCK, 0:BLOCK] = kp[...]
 
+    update_copy = pltpu.make_async_copy(update, update_hbm, local_sem.at[2])
+    update_copy.start()
     wait_pieces(last)
 
     for cond, copy in pending:
@@ -458,10 +506,13 @@
         return carry
 
     lax.fori_loop(0, rb, subtract, 0)
+    child_copy.wait()
+    update_copy.wait()
 
 
 def assemble_kernel(children, sources, where_am_i, update, *refs):
-    blocks, out = refs[:children], refs[children]
+    blocks, same, out, child = refs[:children], *refs[children:]
+    child[...] = same[...]
     r = pl.program_id(0)
     for c in range(out.shape[1] // BLOCK):
         span = slice(c * BLOCK, (c + 1) * BLOCK)
@@ -488,12 +539,12 @@
         grid_spec=pltpu.PrefetchScalarGridSpec(
             num_scalar_prefetch=2,
             grid=(height // BLOCK,),
-            in_specs=[row] + [pl.BlockSpec((BLOCK, breadth), moved(s)) for s in range(children)],
-            out_specs=row,
+            in_specs=[row] + [pl.BlockSpec((BLOCK, breadth), moved(s)) for s in range(children)] + [row],
+            out_specs=(row, row),
         ),
-        out_shape=jax.ShapeDtypeStruct((height, breadth), jnp.float32),
+        out_shape=(jax.ShapeDtypeStruct((height, breadth), jnp.float32),) * 2,
         name="assemble",
-    )(sources, where_am_i, update, *blocks)
+    )(sources, where_am_i, update, *blocks, blocks[0])
 
 
 def per_device(sizes, child_fronts, parent_front, block_maps):
@@ -522,7 +573,7 @@
     )
     f32 = jnp.float32
     block = jax.ShapeDtypeStruct((height, breadth), f32)
-    vmem = pl.BlockSpec(memory_space=pltpu.VMEM)
+    vmem, away = pl.BlockSpec(memory_space=pltpu.VMEM), pl.BlockSpec(memory_space=pl.ANY)
     sends = (
         leaves * (frows - 1) + 2 * fcols + leaves * CHUNKS * 2 + leaves * fcols + leaves * 7
         + frows + fcols * 3 + 4 + fcols * leaves
@@ -547,8 +598,14 @@
         pltpu.VMEM(square, f32),
         pltpu.VMEM((height, BLOCK), f32),
         pltpu.VMEM((BLOCK, breadth), f32),
+        pltpu.VMEM((height, breadth), f32),
+        pltpu.VMEM((height, breadth), f32),
+        pltpu.VMEM((height, breadth), f32),
+        pltpu.VMEM((WIDE, breadth), jnp.bfloat16),
+        pltpu.VMEM((WIDE, breadth), jnp.bfloat16),
         pltpu.SemaphoreType.DMA((sends,)),
         pltpu.SemaphoreType.DMA((leaves * 14 + 10,)),
+        pltpu.SemaphoreType.DMA((3,)),
     ]
     child, other, update, tables = pl.pallas_call(
         functools.partial(kernel, sizes),
@@ -558,8 +615,8 @@
             block,
             jax.ShapeDtypeStruct((leaves - 1, 2, deep, BLOCK), jnp.int32),
         ),
-        in_specs=[vmem] * 4,
-        out_specs=(vmem,) * 4,
+        in_specs=[vmem] * 3 + [away],
+        out_specs=(away, vmem, away, vmem),
         scratch_shapes=scratch,
         compiler_params=pltpu.CompilerParams(
             collective_id=0, has_side_effects=True, vmem_limit_bytes=56 * 2**20
@@ -568,7 +625,7 @@
     )(table, table_send, child_fronts[0], parent_front)
     sources = jnp.concatenate([table[None], tables], axis=0)[:, :, :, 0]
     where_am_i = jnp.stack([i, j]).astype(jnp.int32)
-    parent = assemble(sources, where_am_i, update, [child] + [other[s] for s in range(leaves - 1)])
+    parent, child = assemble(sources, where_am_i, update, [child] + [other[s] for s in range(leaves - 1)])
     return child[None], parent
 
 

time: 175 us -> 176 us (level)
  Pallas kernels: 164 us -> 171 us
  local copies, waits for them, and re-layouts: 6.19 us -> 1.41 us
    unnamed x1 -> x0, local copies, waits for them, and re-layouts: 4.79 us -> none
    pallas_call x1, Pallas kernels: 155 us -> 159 us  [per_device(): pl.pallas_call(functools.partial(kernel, sizes), out_shape=(block, jax.Sh...]
    pallas_call x1, Pallas kernels: 9.53 us -> 11.7 us  [assemble(): pl.pallas_call(functools.partial(assemble_kernel, children), grid_spec=pl...]
where the time goes in v3:
time: 176 us
  Pallas kernels  171 us (97%)
  other arithmetic  2.93 us (2%)
    pallas_call x1, Pallas kernels, per_device(): pl.pallas_call(functools.partial(kernel, sizes), out_shape=(block, jax.Sh...  159 us
    pallas_call x1, Pallas kernels, assemble(): pl.pallas_call(functools.partial(assemble_kernel, children), grid_spec=pl...  11.7 us

profile of v3, /device:TPU:31, one launch (start us, length us, event | category | flops | bytes accessed | tf_op | source)
XLA Modules:
  0.0 176.0 jit_solution(1495548849050995078)
XLA Ops:
  0.6 0.7 select_reduce_fusion
  1.4 0.1 fusion.3
  1.5 0.7 pad_add_fusion.3.where_am_i
  2.2 0.7 broadcast_in_dim.46.table_send
  2.8 0.7 broadcast_in_dim.45.table
  3.5 0.1 broadcast_in_dim_broadcast_in_dim.2
  3.6 159.2 %fronts.1 = (f32[1024,1024]{1,0:T(8,128)}, f32[1,1024,1024]{2,1,0:T(8,128)}, f32[1024,1024]{1,0:T(8,128)}, s32[1,2,8,128]{3,2,1,0:T(8,128)}) custom-call(s32[2,8,128]{2,1,0:T(8,128)} %broadcast_in_dim.45.table, s32[2,8,128]{2,1,0:T(8,128)} %broadcast_in_dim.46.table_send, f32[1024,1024]{1,0:T(8,128)} %bitcast.16, f32[1024,1024]{1,0:T(8,128)} %front_hbm.1), custom_call_target="tpu_custom_call" | custom-call | tf_op jit(solution)/shard_map/fronts/pallas_call | solution.py:610
  162.8 1.4 fusion.sources
  164.3 11.7 %assemble.1 = (f32[1024,1024]{1,0:T(8,128)}, f32[1024,1024]{1,0:T(8,128)}) custom-call(s32[2,2,8]{2,1,0:T(2,128)} %fusion.sources, s32[2]{0:T(128)} %pad_add_fusion.3.where_am_i, f32[1024,1024]{1,0:T(8,128)} %get-tuple-element.9.update, f32[1024,1024]{1,0:T(8,128)} %get-tuple-element.10.refs_0_.refs_2_, f32[1024,1024]{1,0:T(8,128)} %bitcast.17, ...), custom_call_target="tpu_custom_call" | custom-call | tf_op jit(solution)/shard_map/assemble/pallas_call | solution.py:537
  (1 shorter events, 0.0 us)

commit v4 on v3

--- a/solution.py
+++ b/solution.py
@@ -149,8 +149,26 @@
     send_pivot(0)
     for q in range(CHUNKS):
         start(top, chunk(own.at[pl.ds(0, WIDE)], q, CHUNKS), chunk(cols.at[0], q, CHUNKS), sem("c", 0, q), up)
-    for c in range(1, fcols):
-        start(first, own.at[:, pl.ds(0, WIDE)], rows.at[0], sem("r", 0), {"fcol": c})
+    half = height // 2
+
+    def send_rows(s, source):
+        for c in range(1, fcols):
+            if c == 1:
+                start(first, source, rows.at[s], sem("r", s), {"fcol": c})
+            else:
+                part = pl.ds(c % 2 * half, half)
+                start(first, source.at[part], rows.at[s, part], sem("r", s), {"fcol": c})
+
+    def take_rows(s):
+        partner = {"fcol": j + 1 - 2 * lax.rem(j, 2)}
+        mine = rows.at[s, pl.ds(pl.multiple_of(lax.rem(j, 2) * half, 8), half)]
+        theirs = rows.at[s, pl.ds(pl.multiple_of((1 - lax.rem(j, 2)) * half, 8), half)]
+        arrived(j == 1, rows.at[s], sem("r", s), root_row)
+        arrived(j > 1, mine, sem("r", s), root_row)
+        start(j > 1, mine, mine, sem("r2", s), partner)
+        arrived(j > 1, theirs, sem("r2", s), partner)
+
+    send_rows(0, own.at[:, pl.ds(0, WIDE)])
 
     def is_at(ref, kind, k, t, shape):
         return jnp.broadcast_to(ref[kind, pl.ds(k, 1), 0:1], shape) == t
@@ -198,10 +216,10 @@
             for s in range(1, leaves):
                 start(cond, piece(source, n), piece(other.at[s - 1], n), sem("y", s, n), leaf_at(s))
 
-    def wait_pieces(numbers):
+    def wait_pieces(numbers, cond=always):
         for n in numbers:
             for s in range(1, leaves):
-                arrived(always, piece(other.at[s - 1], n), sem("y", s, n), leaf_at(leaves - s))
+                arrived(cond, piece(other.at[s - 1], n), sem("y", s, n), leaf_at(leaves - s))
 
     for s in range(1, leaves):
         start(always, table_send, tables.at[s - 1], sem("tables", s), leaf_at(s))
@@ -265,7 +283,9 @@
         arrived(inner_rows, here, sem("c", s, q), down)
         start(inner_rows, here, here, sem("c", s, q), up)
 
-    wait_pieces([0])
+    edge = top | first
+    inside = (i > 0) & (j > 0)
+    wait_pieces([0], edge)
     for s in range(1, leaves):
         send_pivot(s)
     for s in range(1, leaves):
@@ -286,7 +306,7 @@
             for s in range(1, leaves):
                 pass_cols(s, q)
         if n == CHUNKS - 1:
-            wait_pieces([1])
+            wait_pieces([1], top)
             for s in range(1, leaves):
                 for p in range(CHUNKS):
                     source = chunk(other.at[s - 1, pl.ds(0, WIDE)], p, CHUNKS)
@@ -296,10 +316,9 @@
                 def _(s=s):
                     cols[s] = other[s - 1, 0:WIDE, :]
         if n == CHUNKS + 1:
-            wait_pieces(panel)
+            wait_pieces(panel, first)
             for s in range(1, leaves):
-                for c in range(1, fcols):
-                    start(first, other.at[s - 1, :, pl.ds(0, WIDE)], rows.at[s], sem("r", s), {"fcol": c})
+                send_rows(s, other.at[s - 1, :, pl.ds(0, WIDE)])
 
                 @pl.when(first)
                 def _(s=s):
@@ -329,7 +348,7 @@
         arrived(always, tables.at[s - 1], sem("tables", s), leaf_at(leaves - s))
 
     def make_panels(s):
-        arrived(j > 0, rows.at[s], sem("r", s), root_row)
+        take_rows(s)
         for q in range(CHUNKS):
             arrived(i == frows - 1, chunk(cols.at[s], q, CHUNKS), sem("c", s, q), down)
 
@@ -369,7 +388,9 @@
     child_copy.start()
     for s in range(1, leaves):
         make_panels(s)
-    wait_pieces(middle)
+    wait_pieces([1], first & (i > 0))
+    wait_pieces(panel, top & (j > 0))
+    wait_pieces(middle, edge)
     load.wait()
 
     third = block_slice(CHILD_PANELS)
@@ -441,8 +462,8 @@
         start(corner, ppiv, ppiv, sem("pp"), {"frow": b})
     for c in range(1, fcols):
         start(corner, ppiv, ppiv, sem("pp"), {"fcol": c})
-    for q in range(2):
-        start(top, chunk(pcol, q, 2), chunk(pcol, q, 2), sem("pc", q), up)
+    for q in range(CHUNKS):
+        start(top, chunk(pcol, q, CHUNKS), chunk(pcol, q, CHUNKS), sem("pc", q), up)
     for c in range(1, fcols):
         start(first, prow, prow, sem("pr"), {"fcol": c})
     arrived(first & (i > 0), ppiv, sem("pp"), down)
@@ -464,15 +485,14 @@
     def pass_parent():
         n = len(turn)
         turn.append(n)
-        if n % 2 == 0:
-            part = chunk(pcol, n // 2, 2)
-            arrived(inner_rows, part, sem("pc", n // 2), down)
-            start(inner_rows, part, part, sem("pc", n // 2), up)
+        part = chunk(pcol, n, CHUNKS)
+        arrived(inner_rows, part, sem("pc", n), down)
+        start(inner_rows, part, part, sem("pc", n), up)
 
     upper, inverse = factor_block(ppiv[...], pass_parent)
     kp[...] = upper.T
-    for q in range(2):
-        arrived(i == frows - 1, chunk(pcol, q, 2), sem("pc", q), down)
+    for q in range(CHUNKS):
+        arrived(i == frows - 1, chunk(pcol, q, CHUNKS), sem("pc", q), down)
     arrived(j > 0, prow, sem("pr"), root_row)
     lprow[...] = dot_t(prow[...], inverse)
     lpcol[...] = dot(inverse, pcol[...])
@@ -495,6 +515,10 @@
 
     update_copy = pltpu.make_async_copy(update, update_hbm, local_sem.at[2])
     update_copy.start()
+    wait_pieces([0], inside)
+    wait_pieces([1], inside)
+    wait_pieces(panel, inside)
+    wait_pieces(middle, inside)
     wait_pieces(last)
 
     for cond, copy in pending:
@@ -550,7 +574,7 @@
 def per_device(sizes, child_fronts, parent_front, block_maps):
     leaves, frows, fcols = sizes
     height, breadth = parent_front.shape
-    assert fcols % leaves == 0
+    assert fcols % leaves == 0 and fcols % 2 == 0
     rb, cb = height // BLOCK, breadth // BLOCK
     i, j = lax.axis_index("frow"), lax.axis_index("fcol")
     number = jnp.arange(block_maps.shape[1], dtype=jnp.int32)

time: 176 us -> 177 us (level)
  no operation moved by 1% of the time
where the time goes in v4:
time: 177 us; the launch traced here: 176 us
  Pallas kernels  171 us (97%)
  other arithmetic  2.93 us (2%)
    pallas_call x1, Pallas kernels, per_device(): pl.pallas_call(functools.partial(kernel, sizes), out_shape=(block, jax.Sh...  159 us
    pallas_call x1, Pallas kernels, assemble(): pl.pallas_call(functools.partial(assemble_kernel, children), grid_spec=pl...  11.7 us

profile of v4, /device:TPU:31, one launch (start us, length us, event | category | flops | bytes accessed | tf_op | source)
XLA Modules:
  0.0 176.3 jit_solution(435004899973086734)
XLA Ops:
  0.6 0.7 select_reduce_fusion
  1.4 0.1 fusion.3
  1.5 0.7 pad_add_fusion.3.where_am_i
  2.2 0.7 broadcast_in_dim.46.table_send
  2.8 0.7 broadcast_in_dim.45.table
  3.5 0.1 broadcast_in_dim_broadcast_in_dim.2
  3.6 159.5 %fronts.1 = (f32[1024,1024]{1,0:T(8,128)}, f32[1,1024,1024]{2,1,0:T(8,128)}, f32[1024,1024]{1,0:T(8,128)}, s32[1,2,8,128]{3,2,1,0:T(8,128)}) custom-call(s32[2,8,128]{2,1,0:T(8,128)} %broadcast_in_dim.45.table, s32[2,8,128]{2,1,0:T(8,128)} %broadcast_in_dim.46.table_send, f32[1024,1024]{1,0:T(8,128)} %bitcast.16, f32[1024,1024]{1,0:T(8,128)} %front_hbm.1), custom_call_target="tpu_custom_call" | custom-call | tf_op jit(solution)/shard_map/fronts/pallas_call | solution.py:634
  163.1 1.4 fusion.sources
  164.5 11.7 %assemble.1 = (f32[1024,1024]{1,0:T(8,128)}, f32[1024,1024]{1,0:T(8,128)}) custom-call(s32[2,2,8]{2,1,0:T(2,128)} %fusion.sources, s32[2]{0:T(128)} %pad_add_fusion.3.where_am_i, f32[1024,1024]{1,0:T(8,128)} %get-tuple-element.9.update, f32[1024,1024]{1,0:T(8,128)} %get-tuple-element.10.refs_0_.refs_2_, f32[1024,1024]{1,0:T(8,128)} %bitcast.17, ...), custom_call_target="tpu_custom_call" | custom-call | tf_op jit(solution)/shard_map/assemble/pallas_call | solution.py:561
  (1 shorter events, 0.0 us)

commit v5 on v4

--- a/solution.py
+++ b/solution.py
@@ -256,7 +256,6 @@
     send_pieces([1], i > 0)
     send_pieces(middle, top)
     send_pieces(middle[:1], i > 0)
-    send_pieces(last)
 
     @pl.when(top)
     def _():
@@ -316,6 +315,7 @@
                 def _(s=s):
                     cols[s] = other[s - 1, 0:WIDE, :]
         if n == CHUNKS + 1:
+            send_pieces(last)
             wait_pieces(panel, first)
             for s in range(1, leaves):
                 send_rows(s, other.at[s - 1, :, pl.ds(0, WIDE)])

time: 177 us -> 177 us (level)
  no operation moved by 1% of the time
where the time goes in v5:
time: 177 us; the launch traced here: 176 us
  Pallas kernels  171 us (97%)
  other arithmetic  2.93 us (2%)
    pallas_call x1, Pallas kernels, per_device(): pl.pallas_call(functools.partial(kernel, sizes), out_shape=(block, jax.Sh...  159 us
    pallas_call x1, Pallas kernels, assemble(): pl.pallas_call(functools.partial(assemble_kernel, children), grid_spec=pl...  11.8 us

profile of v5, /device:TPU:31, one launch (start us, length us, event | category | flops | bytes accessed | tf_op | source)
XLA Modules:
  0.0 176.3 jit_solution(13884087008530213637)
XLA Ops:
  0.6 0.7 select_reduce_fusion
  1.4 0.1 fusion.3
  1.5 0.7 pad_add_fusion.3.where_am_i
  2.2 0.7 broadcast_in_dim.46.table_send
  2.8 0.7 broadcast_in_dim.45.table
  3.5 0.1 broadcast_in_dim_broadcast_in_dim.2
  3.6 159.5 %fronts.1 = (f32[1024,1024]{1,0:T(8,128)}, f32[1,1024,1024]{2,1,0:T(8,128)}, f32[1024,1024]{1,0:T(8,128)}, s32[1,2,8,128]{3,2,1,0:T(8,128)}) custom-call(s32[2,8,128]{2,1,0:T(8,128)} %broadcast_in_dim.45.table, s32[2,8,128]{2,1,0:T(8,128)} %broadcast_in_dim.46.table_send, f32[1024,1024]{1,0:T(8,128)} %bitcast.16, f32[1024,1024]{1,0:T(8,128)} %front_hbm.1), custom_call_target="tpu_custom_call" | custom-call | tf_op jit(solution)/shard_map/fronts/pallas_call | solution.py:634
  163.1 1.4 fusion.sources
  164.5 11.8 %assemble.1 = (f32[1024,1024]{1,0:T(8,128)}, f32[1024,1024]{1,0:T(8,128)}) custom-call(s32[2,2,8]{2,1,0:T(2,128)} %fusion.sources, s32[2]{0:T(128)} %pad_add_fusion.3.where_am_i, f32[1024,1024]{1,0:T(8,128)} %get-tuple-element.9.update, f32[1024,1024]{1,0:T(8,128)} %get-tuple-element.10.refs_0_.refs_2_, f32[1024,1024]{1,0:T(8,128)} %bitcast.17, ...), custom_call_target="tpu_custom_call" | custom-call | tf_op jit(solution)/shard_map/assemble/pallas_call | solution.py:561
  (1 shorter events, 0.0 us)
